TPU v7x, 512 devices: a whole 4x8x8 slice. The times are simulated.
512 devices in a mesh: gx: 16 (over y_lo, x), gy: 8 (over z), gz: 4 (over y_hi, core).
Axes of the slice: x: 4, y: 8 (y_hi: 2, y_lo: 4; y = y_hi * 4 + y_lo), z: 8, core: 2. Of those that a mesh axis runs over, the one named last changes fastest.
Arguments:
- camera: bfloat16 [6, 512, 128, 256], P(None, 'gx', ('gy', 'gz')), may hold values from 0.19921875 to 3
- initial: float32 [256, 128, 512], P('gx', 'gy', 'gz'), may hold values from 0.5 to 2
- psf_taps: float32 [6, 3, 31], replicated, may hold values from 0.05 to 1
Outputs:
- deconvolved: float32 [256, 128, 512], P('gx', 'gy', 'gz')
All inputs are finite; a program needn't handle non-finite values.
Results may differ from a plain program's by a relative error of at most 0.0006.
Values may be sent and summed in bfloat16 or wider, within the bound.
A program may use at most 64 MiB of HBM per device.

v0:
```python
import jax
import jax.numpy as jnp
from jax import lax
from jax.sharding import PartitionSpec as P

VIEWS = 6
TAPS = 31
ITERS = 2


HIGH = lax.Precision.HIGHEST


def extended(block, sides, width):
    for axis, dim in sides:
        count = lax.axis_size(axis)
        forward = [(i, i + 1) for i in range(count - 1)]
        backward = [(target, source) for source, target in forward]
        low = lax.ppermute(
            lax.slice_in_dim(block, block.shape[dim] - width, None, axis=dim), axis, forward
        )
        high = lax.ppermute(lax.slice_in_dim(block, 0, width, axis=dim), axis, backward)
        block = jnp.concatenate([low, block, high], axis=dim)
    return block


def banded(kernel, length, backward):
    half = TAPS // 2
    rows = jnp.arange(length + 2 * half, dtype=jnp.int32)
    cols = jnp.arange(length, dtype=jnp.int32)
    distance = rows[:, None] - cols[None, :]
    offset_index = distance if backward else 2 * half - distance
    onehot = (offset_index[None, :, :] == jnp.arange(TAPS, dtype=jnp.int32)[:, None, None]).astype(
        jnp.float32
    )
    return jnp.einsum("vt,tji->vji", kernel, onehot, precision=HIGH)


def per_device(camera, initial, psf_taps):
    half = TAPS // 2
    exchanged = lax.all_to_all(
        lax.all_to_all(camera, "gx", split_axis=3, concat_axis=1, tiled=True),
        "gz",
        split_axis=1,
        concat_axis=2,
        tiled=True,
    )
    images = jnp.transpose(exchanged, (0, 3, 2, 1))
    extent_x, extent_y, extent_z = initial.shape
    kernels = psf_taps / jnp.sum(psf_taps, axis=-1, keepdims=True)
    blur_x = banded(kernels[:, 0], extent_x, False)
    blur_y = banded(kernels[:, 1], extent_y, False)
    blur_z = banded(kernels[:, 2], extent_z, False)
    back_x = banded(kernels[:, 0], extent_x, True).astype(jnp.bfloat16)
    back_y = banded(kernels[:, 1], extent_y, True).astype(jnp.bfloat16)
    back_z = banded(kernels[:, 2], extent_z, True).astype(jnp.bfloat16)
    estimate = initial
    for sweep in range(ITERS):
        padded = extended(estimate.astype(jnp.bfloat16), (("gz", 2),), half).astype(estimate.dtype)
        blurred = jnp.einsum("xyj,vji->vxyi", padded, blur_z, precision=HIGH)
        blurred = extended(blurred.astype(jnp.bfloat16), (("gy", 2),), half).astype(blurred.dtype)
        blurred = jnp.einsum("vxjz,vji->vxiz", blurred, blur_y, precision=HIGH)
        blurred = extended(blurred.astype(jnp.bfloat16), (("gx", 1),), half).astype(blurred.dtype)
        blurred = jnp.einsum("vjyz,vji->viyz", blurred, blur_x, precision=HIGH)
        quotient = (images.astype(jnp.float32) / blurred).astype(jnp.bfloat16)
        widened_q = extended(quotient, (("gz", 3),), half)
        third = jnp.einsum(
            "vxyj,vji->vxyi", widened_q, back_z, preferred_element_type=jnp.float32
        ).astype(jnp.bfloat16)
        third = extended(third, (("gy", 2),), half)
        second = jnp.einsum(
            "vxjz,vji->vxiz", third, back_y, preferred_element_type=jnp.float32
        ).astype(jnp.bfloat16)
        second = extended(second, (("gx", 1),), half)
        correction = jnp.einsum(
            "vjyz,vji->viyz", second, back_x, preferred_element_type=jnp.float32
        )
        estimate = estimate * jnp.sum(correction, axis=0) / VIEWS
    return estimate


def solution(mesh):
    in_specs = (P(None, "gx", ("gy", "gz"), None), P("gx", "gy", "gz"), P())
    out_specs = P("gx", "gy", "gz")
    return jax.shard_map(
        per_device, mesh=mesh, in_specs=in_specs, out_specs=out_specs, check_vma=False
    )
```

profile of v0, /device:TPU:312, one launch (start us, length us, event | category | flops | bytes accessed | tf_op | source)
XLA Modules:
  0.0 224.3 jit_solution(432866500169996178)
XLA Ops:
  5.1 7.6 %all-to-all-start = ((bf16[16,2,6144]{2,1,0:T(2,128)(2,1)}), bf16[16,2,6144]{2,1,0:T(2,128)(2,1)S(1)}, u32[]{:S(2)}, u32[]{:S(2)}) async-start(bf16[16,2,6144]{2,1,0:T(2,128)(2,1)} %reshape.67), calls=%async_computation | async-start | bytes 786432 | tf_op jit(solution)/shard_map/all_to_all | solution.py:42
  19.6 6.3 %collective-permute-done = bf16[16,16,15]{2,1,0:T(8,128)(2,1)S(1)} collective-permute-done((bf16[16,16,15]{2,1,0:T(8,128)(2,1)S(1)}, bf16[16,16,15]{2,1,0:T(8,128)(2,1)S(1)}, u32[]{:S(2)}, u32[]{:S(2)}) %collective-permute-start) | collective-permute-done | bytes 7712 | tf_op jit(solution)/shard_map/ppermute | solution.py:19
  28.6 3.9 %collective-permute-start.2 = (bf16[6,16,15,128]{3,2,1,0:T(8,128)(2,1)S(1)}, bf16[6,16,15,128]{3,2,1,0:T(8,128)(2,1)S(1)}, u32[]{:S(2)}, u32[]{:S(2)}) collective-permute-start(bf16[6,16,15,128]{3,2,1,0:T(8,128)(2,1)S(1)} %get-tuple-element.23), channel_id=1, source_target_pairs={{0,4},{4,8},{8,12},{12,16},{16,20},{20,24},{24,28},{1,5},{5,9},{9,... | collective-permute-start | bytes 1105928 | tf_op jit(solution)/shard_map/ppermute | solution.py:19
  42.5 4.4 %copy.116 = bf16[6,16,32,4,16]{4,3,0,2,1:T(4,128)(2,1)S(1)} copy(bf16[6,16,32,4,16]{2,4,1,3,0:T(8,128)(2,1)} %bitcast.93) | data formatting | bytes 786432 | tf_op jit(solution)/shard_map/all_to_all | solution.py:42
  46.9 3.9 %reshape.69 = bf16[4,2,24576]{2,1,0:T(2,128)(2,1)} reshape(bf16[512,6,4,16]{3,2,1,0:T(4,128)(2,1)S(1)} %bitcast.90) | data formatting | bytes 786432
  50.8 7.2 %all-to-all-start.1 = ((bf16[4,2,24576]{2,1,0:T(2,128)(2,1)}), bf16[4,2,24576]{2,1,0:T(2,128)(2,1)}, u32[]{:S(2)}, u32[]{:S(2)}) async-start(bf16[4,2,24576]{2,1,0:T(2,128)(2,1)} %reshape.69), calls=%async_computation.1 | async-start | bytes 786432 | tf_op jit(solution)/shard_map/all_to_all | solution.py:41
  58.1 5.3 %collective-permute-start.5 = (bf16[6,15,16,128]{3,2,1,0:T(8,128)(2,1)S(1)}, bf16[6,15,16,128]{3,2,1,0:T(8,128)(2,1)S(1)}, u32[]{:S(2)}, u32[]{:S(2)}) collective-permute-start(bf16[6,15,16,128]{3,2,1,0:T(8,128)(2,1)S(1)} %get-tuple-element.22), channel_id=1, source_target_pairs={{32,0},{64,32},{96,64},{128,96},{160,128},{192,160},{224,192},{256... | collective-permute-start | bytes 1105928 | tf_op jit(solution)/shard_map/ppermute | solution.py:22
  67.5 6.0 %collective-permute-done.5 = bf16[6,15,16,128]{3,2,1,0:T(8,128)(2,1)S(1)} collective-permute-done((bf16[6,15,16,128]{3,2,1,0:T(8,128)(2,1)S(1)}, bf16[6,15,16,128]{3,2,1,0:T(8,128)(2,1)S(1)}, u32[]{:S(2)}, u32[]{:S(2)}) %collective-permute-start.5) | collective-permute-done | bytes 368672 | tf_op jit(solution)/shard_map/ppermute | solution.py:22
  73.5 4.8 %collective-permute-done.4 = bf16[6,15,16,128]{3,2,1,0:T(8,128)(2,1)S(1)} collective-permute-done((bf16[6,15,16,128]{3,2,1,0:T(8,128)(2,1)S(1)}, bf16[6,15,16,128]{3,2,1,0:T(8,128)(2,1)S(1)}, u32[]{:S(2)}, u32[]{:S(2)}) %collective-permute-start.4) | collective-permute-done | bytes 368672 | tf_op jit(solution)/shard_map/ppermute | solution.py:19
  94.9 11.9 %collective-permute-done.6 = bf16[6,16,16,15]{3,1,2,0:T(8,128)(2,1)S(1)} collective-permute-done((bf16[6,16,16,15]{3,1,2,0:T(8,128)(2,1)S(1)}, bf16[6,16,16,15]{3,1,2,0:T(8,128)(2,1)S(1)}, u32[]{:S(2)}, u32[]{:S(2)}) %collective-permute-start.6) | collective-permute-done | bytes 46112 | tf_op jit(solution)/shard_map/ppermute | solution.py:19
  109.9 3.9 %collective-permute-start.8 = (bf16[6,16,15,128]{3,2,1,0:T(8,128)(2,1)S(1)}, bf16[6,16,15,128]{3,2,1,0:T(8,128)(2,1)S(1)}, u32[]{:S(2)}, u32[]{:S(2)}) collective-permute-start(bf16[6,16,15,128]{3,2,1,0:T(8,128)(2,1)S(1)} %get-tuple-element.17), channel_id=1, source_target_pairs={{0,4},{4,8},{8,12},{12,16},{16,20},{20,24},{24,28},{1,5},{5,9},{9,... | collective-permute-start | bytes 1105928 | tf_op jit(solution)/shard_map/ppermute | solution.py:19
  114.0 3.6 %collective-permute-done.9 = bf16[6,16,15,128]{3,2,1,0:T(8,128)(2,1)S(1)} collective-permute-done((bf16[6,16,15,128]{3,2,1,0:T(8,128)(2,1)S(1)}, bf16[6,16,15,128]{3,2,1,0:T(8,128)(2,1)S(1)}, u32[]{:S(2)}, u32[]{:S(2)}) %collective-permute-start.9) | collective-permute-done | bytes 368672 | tf_op jit(solution)/shard_map/ppermute | solution.py:22
  123.4 3.9 %collective-permute-start.10 = (bf16[6,15,16,128]{3,2,1,0:T(8,128)(2,1)S(1)}, bf16[6,15,16,128]{3,2,1,0:T(8,128)(2,1)S(1)}, u32[]{:S(2)}, u32[]{:S(2)}) collective-permute-start(bf16[6,15,16,128]{3,2,1,0:T(8,128)(2,1)S(1)} %get-tuple-element.15), channel_id=1, source_target_pairs={{0,32},{32,64},{64,96},{96,128},{128,160},{160,192},{192,224},{224... | collective-permute-start | bytes 1105928 | tf_op jit(solution)/shard_map/ppermute | solution.py:19
  130.9 4.0 %collective-permute-done.10 = bf16[6,15,16,128]{3,2,1,0:T(8,128)(2,1)S(1)} collective-permute-done((bf16[6,15,16,128]{3,2,1,0:T(8,128)(2,1)S(1)}, bf16[6,15,16,128]{3,2,1,0:T(8,128)(2,1)S(1)}, u32[]{:S(2)}, u32[]{:S(2)}) %collective-permute-start.10) | collective-permute-done | bytes 368672 | tf_op jit(solution)/shard_map/ppermute | solution.py:19
  139.8 7.2 %collective-permute-done.12 = bf16[16,16,15]{2,0,1:T(8,128)(2,1)S(1)} collective-permute-done((bf16[16,16,15]{2,0,1:T(8,128)(2,1)S(1)}, bf16[16,16,15]{2,0,1:T(8,128)(2,1)S(1)}, u32[]{:S(2)}, u32[]{:S(2)}) %collective-permute-start.12) | collective-permute-done | bytes 7712 | tf_op jit(solution)/shard_map/ppermute | solution.py:19
  149.9 3.9 %collective-permute-start.14 = (bf16[6,16,15,128]{3,2,1,0:T(8,128)(2,1)S(1)}, bf16[6,16,15,128]{3,2,1,0:T(8,128)(2,1)S(1)}, u32[]{:S(2)}, u32[]{:S(2)}) collective-permute-start(bf16[6,16,15,128]{3,2,1,0:T(8,128)(2,1)S(1)} %get-tuple-element.13), channel_id=1, source_target_pairs={{0,4},{4,8},{8,12},{12,16},{16,20},{20,24},{24,28},{1,5},{5,9},{9,... | collective-permute-start | bytes 1105928 | tf_op jit(solution)/shard_map/ppermute | solution.py:19
  153.8 3.8 %collective-permute-done.15 = bf16[6,16,15,128]{3,2,1,0:T(8,128)(2,1)S(1)} collective-permute-done((bf16[6,16,15,128]{3,2,1,0:T(8,128)(2,1)S(1)}, bf16[6,16,15,128]{3,2,1,0:T(8,128)(2,1)S(1)}, u32[]{:S(2)}, u32[]{:S(2)}) %collective-permute-start.15) | collective-permute-done | bytes 368672 | tf_op jit(solution)/shard_map/ppermute | solution.py:22
  163.6 3.9 %collective-permute-start.16 = (bf16[6,15,16,128]{3,2,1,0:T(8,128)(2,1)S(1)}, bf16[6,15,16,128]{3,2,1,0:T(8,128)(2,1)S(1)}, u32[]{:S(2)}, u32[]{:S(2)}) collective-permute-start(bf16[6,15,16,128]{3,2,1,0:T(8,128)(2,1)S(1)} %get-tuple-element.11), channel_id=1, source_target_pairs={{0,32},{32,64},{64,96},{96,128},{128,160},{160,192},{192,224},{224... | collective-permute-start | bytes 1105928 | tf_op jit(solution)/shard_map/ppermute | solution.py:19
  171.0 4.0 %collective-permute-done.16 = bf16[6,15,16,128]{3,2,1,0:T(8,128)(2,1)S(1)} collective-permute-done((bf16[6,15,16,128]{3,2,1,0:T(8,128)(2,1)S(1)}, bf16[6,15,16,128]{3,2,1,0:T(8,128)(2,1)S(1)}, u32[]{:S(2)}, u32[]{:S(2)}) %collective-permute-start.16) | collective-permute-done | bytes 368672 | tf_op jit(solution)/shard_map/ppermute | solution.py:19
  183.3 11.9 %collective-permute-done.18 = bf16[6,16,16,15]{3,1,2,0:T(8,128)(2,1)S(1)} collective-permute-done((bf16[6,16,16,15]{3,1,2,0:T(8,128)(2,1)S(1)}, bf16[6,16,16,15]{3,1,2,0:T(8,128)(2,1)S(1)}, u32[]{:S(2)}, u32[]{:S(2)}) %collective-permute-start.18) | collective-permute-done | bytes 46112 | tf_op jit(solution)/shard_map/ppermute | solution.py:19
  198.2 3.9 %collective-permute-start.20 = (bf16[6,16,15,128]{3,2,1,0:T(8,128)(2,1)S(1)}, bf16[6,16,15,128]{3,2,1,0:T(8,128)(2,1)S(1)}, u32[]{:S(2)}, u32[]{:S(2)}) collective-permute-start(bf16[6,16,15,128]{3,2,1,0:T(8,128)(2,1)S(1)} %get-tuple-element.7), channel_id=1, source_target_pairs={{0,4},{4,8},{8,12},{12,16},{16,20},{20,24},{24,28},{1,5},{5,9},{9,... | collective-permute-start | bytes 1105928 | tf_op jit(solution)/shard_map/ppermute | solution.py:19
  202.1 3.8 %collective-permute-done.21 = bf16[6,16,15,128]{3,2,1,0:T(8,128)(2,1)S(1)} collective-permute-done((bf16[6,16,15,128]{3,2,1,0:T(8,128)(2,1)S(1)}, bf16[6,16,15,128]{3,2,1,0:T(8,128)(2,1)S(1)}, u32[]{:S(2)}, u32[]{:S(2)}) %collective-permute-start.21) | collective-permute-done | bytes 368672 | tf_op jit(solution)/shard_map/ppermute | solution.py:22
  211.6 3.9 %collective-permute-start.22 = (bf16[6,15,16,128]{3,2,1,0:T(8,128)(2,1)S(1)}, bf16[6,15,16,128]{3,2,1,0:T(8,128)(2,1)S(1)}, u32[]{:S(2)}, u32[]{:S(2)}) collective-permute-start(bf16[6,15,16,128]{3,2,1,0:T(8,128)(2,1)S(1)} %get-tuple-element.5), channel_id=1, source_target_pairs={{0,32},{32,64},{64,96},{96,128},{128,160},{160,192},{192,224},{224... | collective-permute-start | bytes 1105928 | tf_op jit(solution)/shard_map/ppermute | solution.py:19
  219.1 4.0 %collective-permute-done.22 = bf16[6,15,16,128]{3,2,1,0:T(8,128)(2,1)S(1)} collective-permute-done((bf16[6,15,16,128]{3,2,1,0:T(8,128)(2,1)S(1)}, bf16[6,15,16,128]{3,2,1,0:T(8,128)(2,1)S(1)}, u32[]{:S(2)}, u32[]{:S(2)}) %collective-permute-start.22) | collective-permute-done | bytes 368672 | tf_op jit(solution)/shard_map/ppermute | solution.py:19
  (108 shorter events, 96.3 us)
Async XLA Ops:
  5.1 35.2 %all-to-all-start = ((bf16[16,2,6144]{2,1,0:T(2,128)(2,1)}), bf16[16,2,6144]{2,1,0:T(2,128)(2,1)S(1)}, u32[]{:S(2)}, u32[]{:S(2)}) async-start(bf16[16,2,6144]{2,1,0:T(2,128)(2,1)} %reshape.67), calls=%async_computation | async-start | bytes 786432 | tf_op jit(solution)/shard_map/all_to_all | solution.py:42
  16.4 9.5 %collective-permute-start = (bf16[16,16,15]{2,1,0:T(8,128)(2,1)S(1)}, bf16[16,16,15]{2,1,0:T(8,128)(2,1)S(1)}, u32[]{:S(2)}, u32[]{:S(2)}) collective-permute-start(bf16[16,16,15]{2,1,0:T(8,128)(2,1)S(1)} %get-tuple-element.27), channel_id=1, source_target_pairs={{0,1},{1,2},{2,3},{4,5},{5,6},{6,7},{8,9},{9,10},{10,11},{12,13},{... | collective-permute-start | bytes 23048 | tf_op jit(solution)/shard_map/ppermute | solution.py:19
  26.6 9.7 %collective-permute-start.3 = (bf16[6,16,15,128]{3,2,1,0:T(8,128)(2,1)S(1)}, bf16[6,16,15,128]{3,2,1,0:T(8,128)(2,1)S(1)}, u32[]{:S(2)}, u32[]{:S(2)}) collective-permute-start(bf16[6,16,15,128]{3,2,1,0:T(8,128)(2,1)S(1)} %get-tuple-element.24), channel_id=1, source_target_pairs={{4,0},{8,4},{12,8},{16,12},{20,16},{24,20},{28,24},{5,1},{9,5},{13... | collective-permute-start | bytes 1105928 | tf_op jit(solution)/shard_map/ppermute | solution.py:22
  28.6 10.9 %collective-permute-start.2 = (bf16[6,16,15,128]{3,2,1,0:T(8,128)(2,1)S(1)}, bf16[6,16,15,128]{3,2,1,0:T(8,128)(2,1)S(1)}, u32[]{:S(2)}, u32[]{:S(2)}) collective-permute-start(bf16[6,16,15,128]{3,2,1,0:T(8,128)(2,1)S(1)} %get-tuple-element.23), channel_id=1, source_target_pairs={{0,4},{4,8},{8,12},{12,16},{16,20},{20,24},{24,28},{1,5},{5,9},{9,... | collective-permute-start | bytes 1105928 | tf_op jit(solution)/shard_map/ppermute | solution.py:19
  50.8 28.6 %all-to-all-start.1 = ((bf16[4,2,24576]{2,1,0:T(2,128)(2,1)}), bf16[4,2,24576]{2,1,0:T(2,128)(2,1)}, u32[]{:S(2)}, u32[]{:S(2)}) async-start(bf16[4,2,24576]{2,1,0:T(2,128)(2,1)} %reshape.69), calls=%async_computation.1 | async-start | bytes 786432 | tf_op jit(solution)/shard_map/all_to_all | solution.py:41
  58.1 15.3 %collective-permute-start.5 = (bf16[6,15,16,128]{3,2,1,0:T(8,128)(2,1)S(1)}, bf16[6,15,16,128]{3,2,1,0:T(8,128)(2,1)S(1)}, u32[]{:S(2)}, u32[]{:S(2)}) collective-permute-start(bf16[6,15,16,128]{3,2,1,0:T(8,128)(2,1)S(1)} %get-tuple-element.22), channel_id=1, source_target_pairs={{32,0},{64,32},{96,64},{128,96},{160,128},{192,160},{224,192},{256... | collective-permute-start | bytes 1105928 | tf_op jit(solution)/shard_map/ppermute | solution.py:22
  63.4 14.9 %collective-permute-start.4 = (bf16[6,15,16,128]{3,2,1,0:T(8,128)(2,1)S(1)}, bf16[6,15,16,128]{3,2,1,0:T(8,128)(2,1)S(1)}, u32[]{:S(2)}, u32[]{:S(2)}) collective-permute-start(bf16[6,15,16,128]{3,2,1,0:T(8,128)(2,1)S(1)} %get-tuple-element.21), channel_id=1, source_target_pairs={{0,32},{32,64},{64,96},{96,128},{128,160},{160,192},{192,224},{224... | collective-permute-start | bytes 1105928 | tf_op jit(solution)/shard_map/ppermute | solution.py:19
  87.7 7.2 %collective-permute-start.7 = (bf16[6,16,16,15]{3,1,2,0:T(8,128)(2,1)S(1)}, bf16[6,16,16,15]{3,1,2,0:T(8,128)(2,1)S(1)}, u32[]{:S(2)}, u32[]{:S(2)}) collective-permute-start(bf16[6,16,16,15]{3,1,2,0:T(8,128)(2,1)S(1)} %get-tuple-element.20), channel_id=1, source_target_pairs={{1,0},{2,1},{3,2},{5,4},{6,5},{7,6},{9,8},{10,9},{11,10},{13,12},{... | collective-permute-start | bytes 138248 | tf_op jit(solution)/shard_map/ppermute | solution.py:22
  89.7 17.2 %collective-permute-start.6 = (bf16[6,16,16,15]{3,1,2,0:T(8,128)(2,1)S(1)}, bf16[6,16,16,15]{3,1,2,0:T(8,128)(2,1)S(1)}, u32[]{:S(2)}, u32[]{:S(2)}) collective-permute-start(bf16[6,16,16,15]{3,1,2,0:T(8,128)(2,1)S(1)} %get-tuple-element.19), channel_id=1, source_target_pairs={{0,1},{1,2},{2,3},{4,5},{5,6},{6,7},{8,9},{9,10},{10,11},{12,13},{... | collective-permute-start | bytes 138248 | tf_op jit(solution)/shard_map/ppermute | solution.py:19
  107.9 9.7 %collective-permute-start.9 = (bf16[6,16,15,128]{3,2,1,0:T(8,128)(2,1)S(1)}, bf16[6,16,15,128]{3,2,1,0:T(8,128)(2,1)S(1)}, u32[]{:S(2)}, u32[]{:S(2)}) collective-permute-start(bf16[6,16,15,128]{3,2,1,0:T(8,128)(2,1)S(1)} %get-tuple-element.18), channel_id=1, source_target_pairs={{4,0},{8,4},{12,8},{16,12},{20,16},{24,20},{28,24},{5,1},{9,5},{13... | collective-permute-start | bytes 1105928 | tf_op jit(solution)/shard_map/ppermute | solution.py:22
  109.9 10.9 %collective-permute-start.8 = (bf16[6,16,15,128]{3,2,1,0:T(8,128)(2,1)S(1)}, bf16[6,16,15,128]{3,2,1,0:T(8,128)(2,1)S(1)}, u32[]{:S(2)}, u32[]{:S(2)}) collective-permute-start(bf16[6,16,15,128]{3,2,1,0:T(8,128)(2,1)S(1)} %get-tuple-element.17), channel_id=1, source_target_pairs={{0,4},{4,8},{8,12},{12,16},{16,20},{20,24},{24,28},{1,5},{5,9},{9,... | collective-permute-start | bytes 1105928 | tf_op jit(solution)/shard_map/ppermute | solution.py:19
  121.3 9.5 %collective-permute-start.11 = (bf16[6,15,16,128]{3,2,1,0:T(8,128)(2,1)S(1)}, bf16[6,15,16,128]{3,2,1,0:T(8,128)(2,1)S(1)}, u32[]{:S(2)}, u32[]{:S(2)}) collective-permute-start(bf16[6,15,16,128]{3,2,1,0:T(8,128)(2,1)S(1)} %get-tuple-element.16), channel_id=1, source_target_pairs={{32,0},{64,32},{96,64},{128,96},{160,128},{192,160},{224,192},{256... | collective-permute-start | bytes 1105928 | tf_op jit(solution)/shard_map/ppermute | solution.py:22
  123.4 11.5 %collective-permute-start.10 = (bf16[6,15,16,128]{3,2,1,0:T(8,128)(2,1)S(1)}, bf16[6,15,16,128]{3,2,1,0:T(8,128)(2,1)S(1)}, u32[]{:S(2)}, u32[]{:S(2)}) collective-permute-start(bf16[6,15,16,128]{3,2,1,0:T(8,128)(2,1)S(1)} %get-tuple-element.15), channel_id=1, source_target_pairs={{0,32},{32,64},{64,96},{96,128},{128,160},{160,192},{192,224},{224... | collective-permute-start | bytes 1105928 | tf_op jit(solution)/shard_map/ppermute | solution.py:19
  137.4 9.6 %collective-permute-start.12 = (bf16[16,16,15]{2,0,1:T(8,128)(2,1)S(1)}, bf16[16,16,15]{2,0,1:T(8,128)(2,1)S(1)}, u32[]{:S(2)}, u32[]{:S(2)}) collective-permute-start(bf16[16,16,15]{2,0,1:T(8,128)(2,1)S(1)} %get-tuple-element.25), channel_id=1, source_target_pairs={{0,1},{1,2},{2,3},{4,5},{5,6},{6,7},{8,9},{9,10},{10,11},{12,13},{... | collective-permute-start | bytes 23048 | tf_op jit(solution)/shard_map/ppermute | solution.py:19
  147.9 9.7 %collective-permute-start.15 = (bf16[6,16,15,128]{3,2,1,0:T(8,128)(2,1)S(1)}, bf16[6,16,15,128]{3,2,1,0:T(8,128)(2,1)S(1)}, u32[]{:S(2)}, u32[]{:S(2)}) collective-permute-start(bf16[6,16,15,128]{3,2,1,0:T(8,128)(2,1)S(1)} %get-tuple-element.14), channel_id=1, source_target_pairs={{4,0},{8,4},{12,8},{16,12},{20,16},{24,20},{28,24},{5,1},{9,5},{13... | collective-permute-start | bytes 1105928 | tf_op jit(solution)/shard_map/ppermute | solution.py:22
  149.9 10.9 %collective-permute-start.14 = (bf16[6,16,15,128]{3,2,1,0:T(8,128)(2,1)S(1)}, bf16[6,16,15,128]{3,2,1,0:T(8,128)(2,1)S(1)}, u32[]{:S(2)}, u32[]{:S(2)}) collective-permute-start(bf16[6,16,15,128]{3,2,1,0:T(8,128)(2,1)S(1)} %get-tuple-element.13), channel_id=1, source_target_pairs={{0,4},{4,8},{8,12},{12,16},{16,20},{20,24},{24,28},{1,5},{5,9},{9,... | collective-permute-start | bytes 1105928 | tf_op jit(solution)/shard_map/ppermute | solution.py:19
  161.6 9.4 %collective-permute-start.17 = (bf16[6,15,16,128]{3,2,1,0:T(8,128)(2,1)S(1)}, bf16[6,15,16,128]{3,2,1,0:T(8,128)(2,1)S(1)}, u32[]{:S(2)}, u32[]{:S(2)}) collective-permute-start(bf16[6,15,16,128]{3,2,1,0:T(8,128)(2,1)S(1)} %get-tuple-element.12), channel_id=1, source_target_pairs={{32,0},{64,32},{96,64},{128,96},{160,128},{192,160},{224,192},{256... | collective-permute-start | bytes 1105928 | tf_op jit(solution)/shard_map/ppermute | solution.py:22
  163.6 11.5 %collective-permute-start.16 = (bf16[6,15,16,128]{3,2,1,0:T(8,128)(2,1)S(1)}, bf16[6,15,16,128]{3,2,1,0:T(8,128)(2,1)S(1)}, u32[]{:S(2)}, u32[]{:S(2)}) collective-permute-start(bf16[6,15,16,128]{3,2,1,0:T(8,128)(2,1)S(1)} %get-tuple-element.11), channel_id=1, source_target_pairs={{0,32},{32,64},{64,96},{96,128},{128,160},{160,192},{192,224},{224... | collective-permute-start | bytes 1105928 | tf_op jit(solution)/shard_map/ppermute | solution.py:19
  176.1 7.2 %collective-permute-start.19 = (bf16[6,16,16,15]{3,1,2,0:T(8,128)(2,1)S(1)}, bf16[6,16,16,15]{3,1,2,0:T(8,128)(2,1)S(1)}, u32[]{:S(2)}, u32[]{:S(2)}) collective-permute-start(bf16[6,16,16,15]{3,1,2,0:T(8,128)(2,1)S(1)} %get-tuple-element.10), channel_id=1, source_target_pairs={{1,0},{2,1},{3,2},{5,4},{6,5},{7,6},{9,8},{10,9},{11,10},{13,12},{... | collective-permute-start | bytes 138248 | tf_op jit(solution)/shard_map/ppermute | solution.py:22
  178.0 17.2 %collective-permute-start.18 = (bf16[6,16,16,15]{3,1,2,0:T(8,128)(2,1)S(1)}, bf16[6,16,16,15]{3,1,2,0:T(8,128)(2,1)S(1)}, u32[]{:S(2)}, u32[]{:S(2)}) collective-permute-start(bf16[6,16,16,15]{3,1,2,0:T(8,128)(2,1)S(1)} %get-tuple-element.9), channel_id=1, source_target_pairs={{0,1},{1,2},{2,3},{4,5},{5,6},{6,7},{8,9},{9,10},{10,11},{12,13},{... | collective-permute-start | bytes 138248 | tf_op jit(solution)/shard_map/ppermute | solution.py:19
  196.3 9.7 %collective-permute-start.21 = (bf16[6,16,15,128]{3,2,1,0:T(8,128)(2,1)S(1)}, bf16[6,16,15,128]{3,2,1,0:T(8,128)(2,1)S(1)}, u32[]{:S(2)}, u32[]{:S(2)}) collective-permute-start(bf16[6,16,15,128]{3,2,1,0:T(8,128)(2,1)S(1)} %get-tuple-element.8), channel_id=1, source_target_pairs={{4,0},{8,4},{12,8},{16,12},{20,16},{24,20},{28,24},{5,1},{9,5},{13... | collective-permute-start | bytes 1105928 | tf_op jit(solution)/shard_map/ppermute | solution.py:22
  198.2 10.9 %collective-permute-start.20 = (bf16[6,16,15,128]{3,2,1,0:T(8,128)(2,1)S(1)}, bf16[6,16,15,128]{3,2,1,0:T(8,128)(2,1)S(1)}, u32[]{:S(2)}, u32[]{:S(2)}) collective-permute-start(bf16[6,16,15,128]{3,2,1,0:T(8,128)(2,1)S(1)} %get-tuple-element.7), channel_id=1, source_target_pairs={{0,4},{4,8},{8,12},{12,16},{16,20},{20,24},{24,28},{1,5},{5,9},{9,... | collective-permute-start | bytes 1105928 | tf_op jit(solution)/shard_map/ppermute | solution.py:19
  209.7 9.4 %collective-permute-start.23 = (bf16[6,15,16,128]{3,2,1,0:T(8,128)(2,1)S(1)}, bf16[6,15,16,128]{3,2,1,0:T(8,128)(2,1)S(1)}, u32[]{:S(2)}, u32[]{:S(2)}) collective-permute-start(bf16[6,15,16,128]{3,2,1,0:T(8,128)(2,1)S(1)} %get-tuple-element.6), channel_id=1, source_target_pairs={{32,0},{64,32},{96,64},{128,96},{160,128},{192,160},{224,192},{256... | collective-permute-start | bytes 1105928 | tf_op jit(solution)/shard_map/ppermute | solution.py:22
  211.6 11.5 %collective-permute-start.22 = (bf16[6,15,16,128]{3,2,1,0:T(8,128)(2,1)S(1)}, bf16[6,15,16,128]{3,2,1,0:T(8,128)(2,1)S(1)}, u32[]{:S(2)}, u32[]{:S(2)}) collective-permute-start(bf16[6,15,16,128]{3,2,1,0:T(8,128)(2,1)S(1)} %get-tuple-element.5), channel_id=1, source_target_pairs={{0,32},{32,64},{64,96},{96,128},{128,160},{160,192},{192,224},{224... | collective-permute-start | bytes 1105928 | tf_op jit(solution)/shard_map/ppermute | solution.py:19
  (14 other events, 116.5 us)
where the time goes:
time: 225 us; the launch traced here: 224 us
  waiting for transfers between devices  103 us (46%)
  starting transfers between devices  81.7 us (36%)
  local copies, waits for them, and re-layouts  25.4 us (11%)
  matrix products  10.4 us (5%)
  other arithmetic  3.42 us (2%)
    ppermute x12, waiting for transfers between devices, extended(): lax.ppermute(lax.slice_in_dim(block, block.shape[dim] - width, None, axis...  66.8 us
    ppermute x12, starting transfers between devices, extended(): lax.ppermute(lax.slice_in_dim(block, block.shape[dim] - width, None, axis...  38.7 us
    ppermute x12, waiting for transfers between devices, extended(): lax.ppermute(lax.slice_in_dim(block, 0, width, axis=dim), axis, backward)  35.9 us
    ppermute x12, starting transfers between devices, extended(): lax.ppermute(lax.slice_in_dim(block, 0, width, axis=dim), axis, backward)  28.2 us
    unnamed x29, local copies, waits for them, and re-layouts  14.1 us
    all_to_all x1, starting transfers between devices, per_device(): lax.all_to_all(camera, 'gx', split_axis=3, concat_axis=1, tiled=True)  7.58 us
    all_to_all x1, starting transfers between devices, per_device(): lax.all_to_all(lax.all_to_all(camera, 'gx', split_axis=3, concat_axis=1,...  7.2 us
    all_to_all x2, local copies, waits for them, and re-layouts, per_device(): lax.all_to_all(camera, 'gx', split_axis=3, concat_axis=1, tiled=True)  5.92 us
  transfers between devices with their start and end apart: 26, of which 23 were waited for; matrix products, arithmetic and copies ran while one was open for 3% of the time, Pallas kernels for 0%

commit v1 on v0

v1 whole, which is shorter than its diff:
```python
import functools

import jax
import jax.numpy as jnp
from jax import lax
from jax.experimental import pallas as pl
from jax.experimental.pallas import tpu as pltpu
from jax.sharding import PartitionSpec as P

VIEWS = 6
TAPS = 31
HALF = TAPS // 2
ITERS = 2
F32 = jnp.float32
BF16 = jnp.bfloat16
MESH = pl.DeviceIdType.MESH


def dot(a, b):
    return jnp.dot(a, b, preferred_element_type=F32)


def iota(shape, dim):
    return lax.broadcasted_iota(jnp.int32, shape, dim)


def pick(table, index):
    index = jnp.where((index >= 0) & (index < TAPS), index, 127)
    return jnp.take_along_axis(table, index, axis=1)


def kernel(
    sizes, cam_ref, init_ref, taps_ref, out_ref,
    est, ext, quot, ubuf, kf, kb, bzf, bzb, raw, back, xf, yf, xb, yb, scale,
    picked, place, cam_out, cam_in, cam, third, part, flat, acc, code_out, code_in,
    cam_send, cam_recv, z_send, z_recv, e_send, e_recv, h_send, h_recv,
    q_send, q_recv, c_send, c_recv,
):
    nx, ny, nz = sizes
    gx, gy, gz = lax.axis_index("gx"), lax.axis_index("gy"), lax.axis_index("gz")

    def place_of(n):
        return gx + n // 3 - 1, gy + n % 3 - 1, gz

    def there(n):
        x, y, _ = place_of(n)
        return (x >= 0) & (x < nx) & (y >= 0) & (y < ny)

    def around(body):
        def step(i, carry):
            n = jnp.where(i >= 4, i + 1, i)

            @pl.when(there(n))
            def _():
                body(n)

            return carry

        lax.fori_loop(0, 8, step, 0)

    below, above = gz > 0, gz < nz - 1

    def camera_source(s):
        return 4 * gz + s // 4, gy, s % 4

    def camera_target(a):
        return a, gy, gx // 4

    def is_self(place):
        return (place[0] == gx) & (place[2] == gz)

    own_source = gx // 4 == gz
    barrier = pltpu.get_barrier_semaphore()

    def greet(place):
        pl.semaphore_signal(barrier, inc=1, device_id=place, device_id_type=MESH)

    around(lambda n: greet(place_of(n)))

    @pl.when(below)
    def _():
        greet((gx, gy, gz - 1))

    @pl.when(above)
    def _():
        greet((gx, gy, gz + 1))

    def greet_source(s, carry):
        @pl.when(jnp.logical_not(is_self(camera_source(s))))
        def _():
            greet(camera_source(s))

        return carry

    lax.fori_loop(0, 16, greet_source, 0)

    def clear(i, carry):
        n = jnp.where(i >= 4, i + 1, i)

        @pl.when(jnp.logical_not(there(n)))
        def _():
            lanes = pl.ds(pl.multiple_of(n * 256, 256), 256)
            for it in range(ITERS):
                ext[it, :, lanes] = jnp.zeros((160, 256), BF16)

        return carry

    lax.fori_loop(0, 8, clear, 0)
    for it in range(ITERS):
        @pl.when(jnp.logical_not(below))
        def _():
            ext[it, 128:144, 1024:1280] = jnp.zeros((16, 256), BF16)
            quot[it, :, 128:144, :] = jnp.zeros((VIEWS, 16, 256), BF16)

        @pl.when(jnp.logical_not(above))
        def _():
            ext[it, 144:160, 1024:1280] = jnp.zeros((16, 256), BF16)
            quot[it, :, 144:160, :] = jnp.zeros((VIEWS, 16, 256), BF16)

        quot[it, :, 160:256, :] = jnp.zeros((VIEWS, 96, 256), BF16)
    ubuf[160:256, :] = jnp.zeros((96, 256), BF16)
    ubuf[416:512, :] = jnp.zeros((96, 256), BF16)

    for y in range(16):
        flat[y * 16 : (y + 1) * 16, :] = init_ref[pl.ds(y, 16, stride=16), :]
    est[...] = flat[...].T
    ext[0, 0:128, 1024:1280] = est[...].astype(BF16)

    neighbours = jnp.int32(0)
    for n in range(9):
        if n != 4:
            neighbours += there(n).astype(jnp.int32)
    neighbours += below.astype(jnp.int32) + above.astype(jnp.int32)
    pl.semaphore_wait(barrier, neighbours + 16 - own_source.astype(jnp.int32))

    def ext_lanes(n):
        return pl.ds(pl.multiple_of(n * 256, 256), 256)

    def z_copy(it, up):
        source = 112 if up else 0
        target = 128 if up else 144
        return pltpu.make_async_remote_copy(
            src_ref=ext.at[it, pl.ds(source, 16), pl.ds(1024, 256)],
            dst_ref=ext.at[it, pl.ds(target, 16), pl.ds(1024, 256)],
            send_sem=z_send.at[it, int(up)],
            recv_sem=z_recv.at[it, int(up)],
            device_id=(gx, gy, gz + 1 if up else gz - 1),
            device_id_type=MESH,
        )

    def e_copy(it, n, slot, first, count, sends, recvs):
        return pltpu.make_async_remote_copy(
            src_ref=ext.at[it, pl.ds(first, count), pl.ds(1024, 256)],
            dst_ref=ext.at[it, pl.ds(first, count), ext_lanes(slot)],
            send_sem=sends.at[it, n],
            recv_sem=recvs.at[it, slot],
            device_id=place_of(n),
            device_id_type=MESH,
        )

    def main_copy(it, n, slot):
        return e_copy(it, n, slot, 0, 128, e_send, e_recv)

    def rim_copy(it, n, slot):
        return e_copy(it, n, slot, 128, 32, h_send, h_recv)

    def q_copy(it, up):
        source = 112 if up else 0
        target = 128 if up else 144
        return pltpu.make_async_remote_copy(
            src_ref=quot.at[it, :, pl.ds(source, 16), :],
            dst_ref=quot.at[it, :, pl.ds(target, 16), :],
            send_sem=q_send.at[it, int(up)],
            recv_sem=q_recv.at[it, int(up)],
            device_id=(gx, gy, gz + 1 if up else gz - 1),
            device_id_type=MESH,
        )

    def c_copy(it, n, slot):
        return pltpu.make_async_remote_copy(
            src_ref=code_out.at[it, n],
            dst_ref=code_in.at[it, slot],
            send_sem=c_send.at[it, n],
            recv_sem=c_recv.at[it, slot],
            device_id=place_of(n),
            device_id_type=MESH,
        )

    def both(make, act):
        @pl.when(above)
        def _():
            act(make(True))

        @pl.when(below)
        def _():
            act(make(False))

    def both_in(make):
        @pl.when(below)
        def _():
            make(True).wait_recv()

        @pl.when(above)
        def _():
            make(False).wait_recv()

    def start(copy):
        copy.start()

    def send_estimate(it):
        both(lambda up: z_copy(it, up), start)
        around(lambda n: main_copy(it, n, 8 - n).start())

    send_estimate(0)

    place[...] = jnp.zeros(place.shape, BF16)
    row, col = iota((32, 256), 0), iota((32, 256), 1)
    same_x = row == (col >> 7) * 16 + (col & 15)
    for r in range(2):
        turned = ((col >> 6) & 1) == (r + gz) % 2
        for y in range(4):
            ones = (same_x & turned & (((col >> 4) & 3) == y)).astype(F32).astype(BF16)
            for q in range(4):
                first = (r * 4 + y) * 128 + q * 32
                place[q, first : first + 32, :] = ones
    for v in range(VIEWS):
        r, w = v // 3, v % 3
        for y in range(4):
            plane = cam_ref[v, :, y, :]
            for h in range(2):
                picked[h, w * 32 : (w + 1) * 32, (r * 4 + y) * 128 : (r * 4 + y + 1) * 128] = plane[
                    :, h * 128 : (h + 1) * 128
                ]
    for p in range(8):
        block = dot(picked[p // 4], place[p % 4]).astype(BF16)
        cam_out[2 * p] = block[:, 0:128]
        cam_out[2 * p + 1] = block[:, 128:256]

    slot = (gx % 4) * 4 + gz

    def cam_copy(a, s):
        return pltpu.make_async_remote_copy(
            src_ref=cam_out.at[a],
            dst_ref=cam_in.at[s],
            send_sem=cam_send.at[a],
            recv_sem=cam_recv.at[s],
            device_id=camera_target(a),
            device_id_type=MESH,
        )

    def send_camera(a, carry):
        mine = is_self(camera_target(a))

        @pl.when(mine)
        def _():
            cam_in[slot] = cam_out[a]

        @pl.when(jnp.logical_not(mine))
        def _():
            cam_copy(a, slot).start()

        return carry

    lax.fori_loop(0, 16, send_camera, 0)

    raw[...] = jnp.zeros((24, 128), F32)
    for v in range(VIEWS):
        for a in range(3):
            raw[a * 8 + v : a * 8 + v + 1, 0:TAPS] = taps_ref[v, a : a + 1, :]
    total = jnp.sum(raw[...], axis=1, keepdims=True)
    total = jnp.where((iota((24, 1), 0) & 7) < VIEWS, total, 1.0)
    back[...] = (raw[...] / total).astype(BF16).astype(F32)
    fx, fy, fz = raw[0:8, :], raw[8:16, :], raw[16:24, :]
    bx, by = back[0:8, :], back[8:16, :]
    f_sum, b_sum = jnp.zeros((8, 128), F32), jnp.zeros((8, 128), F32)
    for t in range(TAPS):
        f_sum += (fx[:, t : t + 1] * fy).astype(BF16).astype(F32)
        b_sum += (bx[:, t : t + 1] * by).astype(BF16).astype(F32)

    def lanes_sum(a):
        return jnp.sum(a, axis=1, keepdims=True)

    f_scale = lanes_sum(f_sum) * lanes_sum(fz.astype(BF16).astype(F32))
    b_scale = lanes_sum(bx) * lanes_sum(by) / jnp.where(iota((8, 1), 0) < VIEWS, lanes_sum(b_sum), 1.0)
    scale[0:8, :] = jnp.broadcast_to(f_scale, (8, 128))
    scale[8:16, :] = jnp.broadcast_to(b_scale, (8, 128))

    def tables(j, carry):
        rows = pl.ds(pl.multiple_of(j * 8, 8), 8)
        lane = iota((8, 128), 1)
        x = lane & 15
        xf[rows, :] = pick(raw[0:8, :], x + 31 - j)
        xb[rows, :] = pick(back[0:8, :], j - 1 - x)
        for half in range(2):
            y = (lane >> 4) + 8 * half
            lanes = slice(half * 128, (half + 1) * 128)
            yf[rows, lanes] = pick(raw[8:16, :], y + 31 - j)
            yb[rows, lanes] = pick(back[8:16, :], j - 1 - y)
        return carry

    lax.fori_loop(0, 48, tables, 0)

    def products(i, carry):
        v, n = i // 9, i % 9
        dx, dy = n // 3, n % 3
        x_f = xf[pl.ds(dx * 128 + v, 16, stride=8), :]
        x_b = xb[pl.ds((2 - dx) * 128 + v, 16, stride=8), :]
        for y in range(16):
            y_f = yf[pl.ds((dy * 16 + y) * 8 + v, 1), :]
            y_b = yb[pl.ds(((2 - dy) * 16 + y) * 8 + v, 1), :]
            for half in range(2):
                lanes = slice(half * 128, (half + 1) * 128)
                kf[v, pl.ds(pl.multiple_of(n * 256 + y * 16, 16), 16), lanes] = (
                    x_f * y_f[:, lanes]
                ).astype(BF16)
                kb[n, pl.ds(pl.multiple_of(v * 256 + y * 16, 16), 16), lanes] = (
                    x_b * y_b[:, lanes]
                ).astype(BF16)
        return carry

    lax.fori_loop(0, 9 * VIEWS, products, 0)

    def band_block(i, carry):
        v, block = i // 8, i % 8
        rows = pl.ds(pl.multiple_of(block * 16, 16), 16)
        lane = iota((8, 128), 1)
        far = jnp.where(lane < 16, lane - 16, jnp.where(lane < 32, lane + 112, 1024))
        f_row = jnp.broadcast_to(raw[pl.ds(16 + v, 1), :], (8, 128))
        b_row = jnp.broadcast_to(back[pl.ds(16 + v, 1), :], (8, 128))
        for half, z_in in enumerate((lane, far)):
            lanes = slice(half * 128, (half + 1) * 128)
            forward, backward = [], []
            for k in range(2):
                apart = iota((8, 128), 0) + block * 16 + k * 8 - z_in
                forward.append(pick(f_row, apart + HALF))
                backward.append(pick(b_row, HALF - apart))
            bzf[v, rows, lanes] = jnp.concatenate(forward, axis=0).astype(BF16)
            bzb[v, rows, lanes] = jnp.concatenate(backward, axis=0).astype(BF16)
        return carry

    lax.fori_loop(0, 8 * VIEWS, band_block, 0)

    def receive_camera():
        def wait(s, carry):
            @pl.when(jnp.logical_not(is_self(camera_source(s))))
            def _():
                cam_copy(0, s).wait_recv()

            return carry

        lax.fori_loop(0, 16, wait, 0)
        low = iota((32, 128), 1) < 64
        for v in range(VIEWS):
            r, w = v // 3, v % 3
            for z in range(4):
                for t in range(2):
                    even = cam_in[z * 4 + 2 * t, w * 32 : (w + 1) * 32, :].astype(F32)
                    odd = cam_in[z * 4 + 2 * t + 1, w * 32 : (w + 1) * 32, :].astype(F32)
                    if r == 0:
                        block = jnp.where(low, even, odd)
                    else:
                        block = pltpu.roll(jnp.where(low, odd, even), 64, 1)
                    cam[v, z * 32 : (z + 1) * 32, t * 128 : (t + 1) * 128] = block.astype(BF16)

    def sweep(it, carry):
        both_in(lambda up: z_copy(it, up))
        around(lambda n: rim_copy(it, n, 8 - n).start())
        around(lambda n: main_copy(it, n, n).wait_recv())
        around(lambda n: rim_copy(it, n, n).wait_recv())

        @pl.when(it == 0)
        def _():
            receive_camera()

        def forward(v, carry):
            u = dot(ext[it], kf[v])
            high = u.astype(BF16)
            ubuf[0:160, :] = high
            ubuf[256:416, :] = (u - high.astype(F32)).astype(BF16)
            band = bzf[v]
            blurred = dot(jnp.concatenate([band, band], axis=1), ubuf[...])
            factor = scale[pl.ds(v, 1), :]
            factor = jnp.concatenate([factor, factor], axis=1)
            quot[it, v, 0:128, :] = (cam[v].astype(F32) * factor / blurred).astype(BF16)
            return carry

        lax.fori_loop(0, VIEWS, forward, 0)
        both(lambda up: q_copy(it, up), start)
        both_in(lambda up: q_copy(it, up))
        for v in range(VIEWS):
            factor = scale[8 + v : 9 + v, :]
            factor = jnp.concatenate([factor, factor], axis=1)
            third[:, v * 256 : (v + 1) * 256] = (dot(bzb[v], quot[it, v]) * factor).astype(BF16)

        def backward(i, carry):
            n = jnp.where(i >= 4, i + 1, i)

            @pl.when(there(n))
            def _():
                part[0:128, :] = dot(third[...], kb[n])
                base = jnp.concatenate(
                    [part[g * 16 + 8 : g * 16 + 9, :] for g in range(8)], axis=0
                ).astype(BF16).astype(F32)
                code_out[it, n, 128:144, :] = jnp.concatenate(
                    [base, jnp.zeros((8, 256), F32)], axis=0
                ).astype(BF16)
                for g in range(8):
                    rows = slice(g * 16, (g + 1) * 16)
                    code_out[it, n, rows, :] = (part[rows, :] - base[g : g + 1, :]).astype(BF16)
                c_copy(it, n, 8 - n).start()

            return carry

        lax.fori_loop(0, 8, backward, 0)
        acc[...] = dot(third[...], kb[4])

        def collect(n):
            c_copy(it, n, n).wait_recv()
            base = code_in[it, n, 128:144, :].astype(F32)
            for g in range(8):
                rows = slice(g * 16, (g + 1) * 16)
                acc[rows, :] += code_in[it, n, rows, :].astype(F32) + base[g : g + 1, :]

        around(collect)
        est[...] = est[...] * acc[...] / VIEWS

        @pl.when(it < ITERS - 1)
        def _():
            ext[it + 1, 0:128, 1024:1280] = est[...].astype(BF16)
            send_estimate(it + 1)

        return carry

    lax.fori_loop(0, ITERS, sweep, 0)

    flat[...] = est[...].T
    for y in range(16):
        out_ref[pl.ds(y, 16, stride=16), :] = flat[y * 16 : (y + 1) * 16, :]

    def sent(it, carry):
        both(lambda up: z_copy(it, up), lambda copy: copy.wait_send())
        both(lambda up: q_copy(it, up), lambda copy: copy.wait_send())

        def each(n):
            main_copy(it, n, 8 - n).wait_send()
            rim_copy(it, n, 8 - n).wait_send()
            c_copy(it, n, 8 - n).wait_send()

        around(each)
        return carry

    lax.fori_loop(0, ITERS, sent, 0)

    def sent_camera(a, carry):
        @pl.when(jnp.logical_not(is_self(camera_target(a))))
        def _():
            cam_copy(a, slot).wait_send()

        return carry

    lax.fori_loop(0, 16, sent_camera, 0)


def per_device(sizes, camera, initial, psf_taps):
    vmem = pl.BlockSpec(memory_space=pltpu.VMEM)
    dma = pltpu.SemaphoreType.DMA
    rows = initial.reshape(256, 128)
    result = pl.pallas_call(
        functools.partial(kernel, sizes),
        out_shape=jax.ShapeDtypeStruct((256, 128), F32),
        in_specs=[vmem, vmem, vmem],
        out_specs=vmem,
        scratch_shapes=[
            pltpu.VMEM((128, 256), F32),
            pltpu.VMEM((ITERS, 160, 9 * 256), BF16),
            pltpu.VMEM((ITERS, VIEWS, 256, 256), BF16),
            pltpu.VMEM((512, 256), BF16),
            pltpu.VMEM((VIEWS, 9 * 256, 256), BF16),
            pltpu.VMEM((9, VIEWS * 256, 256), BF16),
            pltpu.VMEM((VIEWS, 128, 256), BF16),
            pltpu.VMEM((VIEWS, 128, 256), BF16),
            pltpu.VMEM((24, 128), F32),
            pltpu.VMEM((24, 128), F32),
            pltpu.VMEM((48 * 8, 128), F32),
            pltpu.VMEM((48 * 8, 256), F32),
            pltpu.VMEM((48 * 8, 128), F32),
            pltpu.VMEM((48 * 8, 256), F32),
            pltpu.VMEM((16, 128), F32),
            pltpu.VMEM((2, 96, 1024), BF16),
            pltpu.VMEM((4, 1024, 256), BF16),
            pltpu.VMEM((16, 96, 128), BF16),
            pltpu.VMEM((16, 96, 128), BF16),
            pltpu.VMEM((VIEWS, 128, 256), BF16),
            pltpu.VMEM((128, VIEWS * 256), BF16),
            pltpu.VMEM((128, 256), F32),
            pltpu.VMEM((256, 128), F32),
            pltpu.VMEM((128, 256), F32),
            pltpu.VMEM((ITERS, 9, 144, 256), BF16),
            pltpu.VMEM((ITERS, 9, 144, 256), BF16),
            dma((16,)), dma((16,)),
            dma((ITERS, 2)), dma((ITERS, 2)),
            dma((ITERS, 9)), dma((ITERS, 9)),
            dma((ITERS, 9)), dma((ITERS, 9)),
            dma((ITERS, 2)), dma((ITERS, 2)),
            dma((ITERS, 9)), dma((ITERS, 9)),
        ],
        compiler_params=pltpu.CompilerParams(
            collective_id=0, has_side_effects=True, vmem_limit_bytes=48 * 1024 * 1024
        ),
    )(camera, rows, psf_taps)
    return result.reshape(initial.shape)


def solution(mesh):
    in_specs = (P(None, "gx", ("gy", "gz"), None), P("gx", "gy", "gz"), P())
    out_specs = P("gx", "gy", "gz")
    sizes = tuple(mesh.shape[a] for a in ("gx", "gy", "gz"))
    return jax.shard_map(
        functools.partial(per_device, sizes),
        mesh=mesh, in_specs=in_specs, out_specs=out_specs, check_vma=False,
    )
```

time: 225 us -> 86.4 us (0.38)
  the two profiles are of different devices: /device:TPU:312 before, /device:TPU:137 now
where the time goes in v1:
time: 86.4 us; the launch traced here: 86.2 us
  Pallas kernels  82.9 us (96%)
  local copies, waits for them, and re-layouts  3.26 us (4%)
    pallas_call x1, Pallas kernels, per_device(): pl.pallas_call(functools.partial(kernel, sizes), out_shape=jax.ShapeDtype...  82.9 us
    unnamed x7, local copies, waits for them, and re-layouts  3.26 us

profile of v1, /device:TPU:137, one launch (start us, length us, event | category | flops | bytes accessed | tf_op | source)
XLA Modules:
  0.0 86.2 jit_solution(3784857762122618393)
XLA Ops:
  0.0 0.0 copy-start
  0.0 1.0 %copy-done = bf16[6,32,4,256]{3,2,1,0:T(4,128)(2,1)S(1)} copy-done((bf16[6,32,4,256]{3,2,1,0:T(4,128)(2,1)S(1)}, bf16[6,32,4,256]{3,2,1,0:T(4,128)(2,1)}, u32[]{:S(2)}) %copy-start) | copy-done | bytes 393240
  1.0 0.0 copy-start.1
  1.0 0.9 %copy-done.1 = f32[16,16,128]{2,1,0:T(8,128)S(1)} copy-done((f32[16,16,128]{2,1,0:T(8,128)S(1)}, f32[16,16,128]{2,1,0:T(8,128)}, u32[]{:S(2)}) %copy-start.1) | copy-done | bytes 131096
  1.9 0.0 copy-start.2
  1.9 0.7 copy-done.2
  2.6 82.9 %shard_map.37 = f32[256,128]{1,0:T(8,128)S(1)} custom-call(bf16[6,32,4,256]{3,2,1,0:T(4,128)(2,1)S(1)} %copy-done, f32[256,128]{1,0:T(8,128)S(1)} %bitcast.3, f32[6,3,31]{2,1,0:T(4,128)S(1)} %copy-done.2), custom_call_target="tpu_custom_call" | custom-call | tf_op jit(solution)/shard_map/pallas_call | solution.py:468
  85.6 0.7 copy.5
Async XLA Ops:
  0.0 1.0 %copy-start = (bf16[6,32,4,256]{3,2,1,0:T(4,128)(2,1)S(1)}, bf16[6,32,4,256]{3,2,1,0:T(4,128)(2,1)}, u32[]{:S(2)}) copy-start(bf16[6,32,4,256]{3,2,1,0:T(4,128)(2,1)} %cam_ref.1) | copy-start | bytes 1179652
  1.0 0.9 %copy-start.1 = (f32[16,16,128]{2,1,0:T(8,128)S(1)}, f32[16,16,128]{2,1,0:T(8,128)}, u32[]{:S(2)}) copy-start(f32[16,16,128]{2,1,0:T(8,128)} %param.4) | copy-start | bytes 393220
  1.9 0.7 copy-start.2

commit v2 on v0

v2 whole, which is shorter than its diff:
```python
import functools

import jax
import jax.numpy as jnp
from jax import lax
from jax.experimental import pallas as pl
from jax.experimental.pallas import tpu as pltpu
from jax.sharding import PartitionSpec as P

VIEWS = 6
TAPS = 31
HALF = TAPS // 2
ITERS = 2
F32 = jnp.float32
BF16 = jnp.bfloat16
MESH = pl.DeviceIdType.MESH
ORDER = (0, 2, 6, 8, 1, 3, 5, 7)


def dot(a, b):
    return jnp.dot(a, b, preferred_element_type=F32)


def iota(shape, dim):
    return lax.broadcasted_iota(jnp.int32, shape, dim)


def inside(index):
    return jnp.where((index >= 0) & (index < TAPS), index, 127)


def pick(table, index):
    return jnp.take_along_axis(table, index, axis=1)


def kernel(
    sizes, cam_hbm, init_hbm, taps_hbm, out_ref,
    cam_raw, init_ref, taps_ref, in_sem,
    est, ext, quot, inverse, ubuf, kf, kb, bzf, bzb, raw, back, xf, yf, xb, yb, scale,
    picked, place, cam_out, cam_in, rim_in, cam, third, part, flat, acc, code_out, code_in,
    cam_send, cam_recv, rim_send, rim_recv, e_send, e_recv, c_send, c_recv,
):
    nx, ny, nz = sizes
    gx, gy, gz = lax.axis_index("gx"), lax.axis_index("gy"), lax.axis_index("gz")
    below, above = gz > 0, gz < nz - 1

    fetch = [
        pltpu.make_async_copy(cam_hbm, cam_raw, in_sem.at[0]),
        pltpu.make_async_copy(init_hbm, init_ref, in_sem.at[1]),
        pltpu.make_async_copy(taps_hbm, taps_ref, in_sem.at[2]),
    ]
    for copy in fetch:
        copy.start()

    def place_of(m):
        n = lax.rem(m, 9)
        return gx + lax.div(n, 3) - 1, gy + lax.rem(n, 3) - 1, gz + lax.div(m, 9) - 1

    def there(m):
        x, y, z = place_of(m)
        return (x >= 0) & (x < nx) & (y >= 0) & (y < ny) & (z >= 0) & (z < nz)

    def around(first, last, body):
        def step(m, carry):
            @pl.when(there(m) & (m != 13))
            def _():
                body(m)

            return carry

        lax.fori_loop(first, last, step, 0)

    part_z, part_i = gx // 4, gx % 4

    def is_self(place):
        return (place[0] == gx) & (place[2] == gz)

    def source(s):
        return 4 * gz + s // 4, gy, s % 4

    def low_source(k):
        return 4 * gz - 1, gy, k

    def high_source(k):
        return 4 * gz + 4, gy, k

    def target(a):
        return a, gy, part_z

    gives_low = (part_i == 3) & (part_z < nz - 1)
    gives_high = (part_i == 0) & (part_z > 0)

    def low_target(a):
        return a, gy, part_z + 1

    def high_target(a):
        return a, gy, part_z - 1

    def others(count, place, body):
        def step(s, carry):
            @pl.when(jnp.logical_not(is_self(place(s))))
            def _():
                body(s)

            return carry

        lax.fori_loop(0, count, step, 0)

    barrier = pltpu.get_barrier_semaphore()

    def greet(place):
        pl.semaphore_signal(barrier, inc=1, device_id=place, device_id_type=MESH)

    others(16, source, lambda s: greet(source(s)))

    @pl.when(below)
    def _():
        others(4, low_source, lambda k: greet(low_source(k)))

    @pl.when(above)
    def _():
        others(4, high_source, lambda k: greet(high_source(k)))

    around(0, 27, lambda m: greet(place_of(m)))

    def one(flag):
        return flag.astype(jnp.int32)

    wide = 1 + one(gx > 0) + one(gx < nx - 1)
    tall = 1 + one(gy > 0) + one(gy < ny - 1)
    deep = 1 + one(below) + one(above)
    greetings = wide * tall * deep - 1 + 16 - one(part_z == gz)
    greetings += one(gives_low) * (16 - one(part_z + 1 == gz))
    greetings += one(gives_high) * (16 - one(part_z - 1 == gz))

    with jax.named_scope("zeros"):
        def clear(m, carry):
            @pl.when(jnp.logical_not(there(m)))
            def _():
                lanes = pl.ds(pl.multiple_of(lax.rem(m, 9) * 256, 256), 256)
                for it in range(ITERS):
                    @pl.when(m < 9)
                    def _():
                        ext[it, 128:160, lanes] = jnp.zeros((32, 256), BF16)

                    @pl.when((m >= 9) & (m < 18))
                    def _():
                        ext[it, 0:128, lanes] = jnp.zeros((128, 256), BF16)

                    @pl.when(m >= 18)
                    def _():
                        ext[it, 160:192, lanes] = jnp.zeros((32, 256), BF16)

            return carry

        lax.fori_loop(0, 27, clear, 0)
        quot[:, 160:256, :] = jnp.zeros((VIEWS, 96, 256), BF16)
        place[...] = jnp.zeros(place.shape, BF16)
        raw[...] = jnp.zeros((24, 128), F32)

    with jax.named_scope("sort camera"):
        row, col = iota((32, 256), 0), iota((32, 256), 1)
        same_x = row == (col >> 7) * 16 + (col & 15)
        for r in range(2):
            turned = ((col >> 6) & 1) == (r + gz) % 2
            for y in range(4):
                ones = (same_x & turned & (((col >> 4) & 3) == y)).astype(F32).astype(BF16)
                for q in range(4):
                    first = (r * 4 + y) * 128 + q * 32
                    place[q, first : first + 32, :] = ones
    fetch[0].wait()
    with jax.named_scope("sort camera 2"):
        for v in range(VIEWS):
            r, w = v // 3, v % 3
            for y in range(4):
                plane = cam_raw[v, :, y, :]
                lanes = slice((r * 4 + y) * 128, (r * 4 + y + 1) * 128)
                for h in range(2):
                    picked[h, w * 32 : (w + 1) * 32, lanes] = plane[:, h * 128 : (h + 1) * 128]
        for p in range(8):
            block = dot(picked[p // 4], place[p % 4]).astype(BF16)
            for w in range(3):
                cam_out[2 * p, w] = block[w * 32 : (w + 1) * 32, 0:128]
                cam_out[2 * p + 1, w] = block[w * 32 : (w + 1) * 32, 128:256]

    fetch[1].wait()
    with jax.named_scope("layout in"):
        for y in range(16):
            flat[y * 16 : (y + 1) * 16, :] = init_ref[pl.ds(y, 16, stride=16), :]
        est[...] = flat[...].T
        ext[0, 0:128, 1024:1280] = est[...].astype(BF16)

    with jax.named_scope("entry wait"):
        pl.semaphore_wait(barrier, greetings)

    slot = part_i * 4 + gz

    def cam_copy(a, s):
        return pltpu.make_async_remote_copy(
            src_ref=cam_out.at[a],
            dst_ref=cam_in.at[s],
            send_sem=cam_send.at[a],
            recv_sem=cam_recv.at[s],
            device_id=target(a),
            device_id_type=MESH,
        )

    def rim_copy(high, a, k):
        first = 0 if high else 16
        return pltpu.make_async_remote_copy(
            src_ref=cam_out.at[a, :, pl.ds(first, 16), :],
            dst_ref=rim_in.at[int(high), k],
            send_sem=rim_send.at[int(high), a],
            recv_sem=rim_recv.at[int(high), k],
            device_id=high_target(a) if high else low_target(a),
            device_id_type=MESH,
        )

    with jax.named_scope("send camera"):
        @pl.when(part_z == gz)
        def _():
            cam_in[slot] = cam_out[gx]

        others(16, target, lambda a: cam_copy(a, slot).start())

        @pl.when(gives_low)
        def _():
            @pl.when(part_z + 1 == gz)
            def _():
                rim_in[0, gz] = cam_out[gx, :, 16:32, :]

            others(16, low_target, lambda a: rim_copy(False, a, gz).start())

        @pl.when(gives_high)
        def _():
            @pl.when(part_z - 1 == gz)
            def _():
                rim_in[1, gz] = cam_out[gx, :, 0:16, :]

            others(16, high_target, lambda a: rim_copy(True, a, gz).start())

    def e_copy(it, step, m, at):
        first, count, to = ((0, 32, 160), (0, 128, 0), (96, 32, 128))[step + 1]
        lanes = pl.ds(pl.multiple_of(lax.rem(at, 9) * 256, 256), 256)
        return pltpu.make_async_remote_copy(
            src_ref=ext.at[it, pl.ds(first, count), pl.ds(1024, 256)],
            dst_ref=ext.at[it, pl.ds(to, count), lanes],
            send_sem=e_send.at[it, m],
            recv_sem=e_recv.at[it, at],
            device_id=place_of(m),
            device_id_type=MESH,
        )

    def each_estimate(act):
        for step in (-1, 1, 0):
            around(9 * (step + 1), 9 * (step + 2), lambda m: act(step, m))

    def send_estimate(it):
        each_estimate(lambda step, m: e_copy(it, step, m, 26 - m).start())

    with jax.named_scope("send estimate"):
        send_estimate(0)

    fetch[2].wait()
    with jax.named_scope("taps"):
        for v in range(VIEWS):
            for a in range(3):
                raw[a * 8 + v : a * 8 + v + 1, 0:TAPS] = taps_ref[v, a : a + 1, :]
        total = jnp.sum(raw[...], axis=1, keepdims=True)
        total = jnp.where((iota((24, 1), 0) & 7) < VIEWS, total, 1.0)
        back[...] = (raw[...] / total).astype(BF16).astype(F32)

    with jax.named_scope("tables"):
        def tables(i, carry):
            lane = iota((8, 128), 1)
            for k in range(6):
                j = i * 6 + k
                rows = pl.ds(pl.multiple_of(j * 8, 8), 8)
                x = lane & 15
                xf[rows, :] = pick(raw[0:8, :], inside(x + 31 - j))
                xb[rows, :] = pick(back[0:8, :], inside(j - 1 - x))
                for half in range(2):
                    y = (lane >> 4) + 8 * half
                    yf[half, rows, :] = pick(raw[8:16, :], inside(y + 31 - j))
                    yb[half, rows, :] = pick(back[8:16, :], inside(j - 1 - y))
            return carry

        lax.fori_loop(0, 8, tables, 0)

    def rows_of(table, j, v):
        return table[pl.ds(j * 128 + v, 16, stride=8), :]

    with jax.named_scope("products"):
        def products(i, carry):
            v, n = i // 9, i % 9
            dx, dy = n // 3, n % 3
            x = rows_of(xf, dx, v)
            for half in range(2):
                ys = rows_of(yf.at[half], dy, v)
                for y in range(16):
                    kf[v, pl.ds(pl.multiple_of(n * 256 + y * 16, 16), 16), half * 128 : (half + 1) * 128] = (
                        x * ys[y : y + 1, :]
                    ).astype(BF16)
            return carry

        lax.fori_loop(0, 9 * VIEWS, products, 0)

    with jax.named_scope("bands"):
        def bands(block, carry):
            r = iota((8, 128), 0) + block * 8
            z_out = jnp.where(r < 128, r, jnp.where(r < 144, r - 144, r - 16))
            rows = pl.ds(pl.multiple_of(block * 8, 8), 8)
            for t in range(3):
                lane = iota((8, 128), 1) + t * 128
                lane = jnp.where(lane < 192, lane, lane - 192)
                z_in = jnp.where(lane < 128, lane, jnp.where(lane < 160, lane - 160, lane - 32))
                index = inside(z_out - z_in + HALF)
                for v in range(VIEWS):
                    band_f = jnp.broadcast_to(raw[16 + v : 17 + v, :], (8, 128))
                    bzf[v, rows, t * 128 : (t + 1) * 128] = pick(band_f, index)
            return carry

        lax.fori_loop(0, 20, bands, 0)

        def back_bands(block, carry):
            z_out = iota((8, 128), 0) + block * 8
            rows = pl.ds(pl.multiple_of(block * 8, 8), 8)
            lane = iota((8, 128), 1)
            far = jnp.where(lane < 16, lane - 16, jnp.where(lane < 32, lane + 112, 1024))
            for half, z_in in enumerate((lane, far)):
                index = inside(z_in - z_out + HALF)
                for v in range(VIEWS):
                    band_b = jnp.broadcast_to(back[16 + v : 17 + v, :], (8, 128))
                    bzb[v, rows, half * 128 : (half + 1) * 128] = pick(band_b, index)
            return carry

        lax.fori_loop(0, 16, back_bands, 0)

    with jax.named_scope("scale"):
        fx, fy, fz = raw[0:8, :], raw[8:16, :], raw[16:24, :]
        bx, by = back[0:8, :], back[8:16, :]
        f_sum, b_sum = jnp.zeros((8, 128), F32), jnp.zeros((8, 128), F32)
        for t in range(TAPS):
            f_sum += (fx[:, t : t + 1] * fy).astype(BF16).astype(F32)
            b_sum += (bx[:, t : t + 1] * by).astype(BF16).astype(F32)

        def lanes_sum(a):
            return jnp.sum(a, axis=1, keepdims=True)

        f_scale = lanes_sum(f_sum) * lanes_sum(fz.astype(BF16).astype(F32))
        b_total = jnp.where(iota((8, 1), 0) < VIEWS, lanes_sum(b_sum), 1.0)
        b_scale = lanes_sum(bx) * lanes_sum(by) / b_total
        scale[0:8, :] = jnp.broadcast_to(f_scale, (8, 128))
        scale[8:16, :] = jnp.broadcast_to(b_scale, (8, 128))

    def factor(row):
        value = scale[row : row + 1, :]
        return jnp.concatenate([value, value], axis=1)

    def blur(it):
        for v in range(VIEWS):
            u = dot(ext[it], kf[v])
            high = u.astype(BF16)
            ubuf[v, 0:192, :] = high
            ubuf[v, 192:384, :] = (u - high.astype(F32)).astype(BF16)
        for v in range(VIEWS):
            inverse[v] = factor(v) / dot(bzf[v].astype(BF16), ubuf[v])

    def wait_estimate(it):
        each_estimate(lambda step, m: e_copy(it, step, m, m).wait_recv())

    def quotients():
        row = iota((32, 256), 0)
        seen = jnp.where(row < 16, one(below), one(above)) > 0
        for v in range(VIEWS):
            quot[v, 0:128, :] = (cam[v, 0:128, :].astype(F32) * inverse[v, 0:128, :]).astype(BF16)
            rim = jnp.where(seen, cam[v, 128:160, :].astype(F32) * inverse[v, 128:160, :], 0.0)
            quot[v, 128:160, :] = rim.astype(BF16)

    with jax.named_scope("wait estimate"):
        wait_estimate(0)
    with jax.named_scope("blur"):
        blur(0)

    with jax.named_scope("back products"):
        def back_products(i, carry):
            v, n = i // 9, i % 9
            dx, dy = n // 3, n % 3
            x = rows_of(xb, 2 - dx, v)
            for half in range(2):
                ys = rows_of(yb.at[half], 2 - dy, v)
                for y in range(16):
                    kb[n, pl.ds(pl.multiple_of(v * 256 + y * 16, 16), 16), half * 128 : (half + 1) * 128] = (
                        x * ys[y : y + 1, :]
                    ).astype(BF16)
            return carry

        lax.fori_loop(0, 9 * VIEWS, back_products, 0)

    with jax.named_scope("camera wait"):
        others(16, source, lambda s: cam_copy(0, s).wait_recv())

        @pl.when(below)
        def _():
            others(4, low_source, lambda k: rim_copy(False, 0, k).wait_recv())

        @pl.when(above)
        def _():
            others(4, high_source, lambda k: rim_copy(True, 0, k).wait_recv())

    with jax.named_scope("assemble"):
        def pair(r, even, odd):
            low = iota(even.shape, 1) < 64
            even, odd = even.astype(F32), odd.astype(F32)
            if r == 0:
                return jnp.where(low, even, odd).astype(BF16)
            return pltpu.roll(jnp.where(low, odd, even), 64, 1).astype(BF16)

        for v in range(VIEWS):
            r, w = v // 3, v % 3
            for t in range(2):
                lanes = slice(t * 128, (t + 1) * 128)
                for z in range(4):
                    cam[v, z * 32 : (z + 1) * 32, lanes] = pair(
                        r, cam_in[z * 4 + 2 * t, w], cam_in[z * 4 + 2 * t + 1, w]
                    )
                for high in range(2):
                    cam[v, 128 + high * 16 : 144 + high * 16, lanes] = pair(
                        r, rim_in[high, 2 * t, w], rim_in[high, 2 * t + 1, w]
                    )

    def c_copy(it, n, at):
        return pltpu.make_async_remote_copy(
            src_ref=code_out.at[it, n],
            dst_ref=code_in.at[it, at],
            send_sem=c_send.at[it, n],
            recv_sem=c_recv.at[it, at],
            device_id=place_of(9 + n),
            device_id_type=MESH,
        )

    for it in range(ITERS):
        if it > 0:
            with jax.named_scope("wait estimate 2"):
                wait_estimate(it)
            with jax.named_scope("blur 2"):
                blur(it)
        with jax.named_scope("quotients"):
            quotients()
        with jax.named_scope("third"):
            for v in range(VIEWS):
                value = dot(bzb[v].astype(BF16), quot[v]) * factor(8 + v)
                third[:, v * 256 : (v + 1) * 256] = value.astype(BF16)

        with jax.named_scope("partial sums"):
            for count, n in enumerate(ORDER):
                @pl.when(there(jnp.int32(9 + n)))
                def _():
                    with jax.named_scope("encode"):
                        work = part.at[count % 2]
                        work[...] = dot(third[...], kb[n])
                        base = jnp.concatenate([work[g * 16 + 8 : g * 16 + 9, :] for g in range(8)], axis=0)
                        base = base.astype(BF16).astype(F32)
                        rest = jnp.zeros((8, 256), F32)
                        code_out[it, n, 128:144, :] = jnp.concatenate([base, rest], axis=0).astype(BF16)
                        for g in range(8):
                            rows = slice(g * 16, (g + 1) * 16)
                            code_out[it, n, rows, :] = (work[rows, :] - base[g : g + 1, :]).astype(BF16)
                    c_copy(it, n, 8 - n).start()

        with jax.named_scope("own sum"):
            acc[...] = dot(third[...], kb[4])

        with jax.named_scope("collect"):
            for n in reversed(ORDER):
                @pl.when(there(jnp.int32(9 + n)))
                def _():
                    c_copy(it, n, n).wait_recv()
                    with jax.named_scope("add"):
                        base = code_in[it, n, 128:144, :].astype(F32)
                        for g in range(8):
                            rows = slice(g * 16, (g + 1) * 16)
                            acc[rows, :] += code_in[it, n, rows, :].astype(F32) + base[g : g + 1, :]

        est[...] = est[...] * acc[...] / VIEWS
        if it < ITERS - 1:
            ext[it + 1, 0:128, 1024:1280] = est[...].astype(BF16)
            with jax.named_scope("send estimate 2"):
                send_estimate(it + 1)

    with jax.named_scope("layout out"):
        flat[...] = est[...].T
        for y in range(16):
            out_ref[pl.ds(y, 16, stride=16), :] = flat[y * 16 : (y + 1) * 16, :]

    with jax.named_scope("sent"):
        def sent(it, carry):
            each_estimate(lambda step, m: e_copy(it, step, m, 26 - m).wait_send())
            around(9, 18, lambda m: c_copy(it, m - 9, 17 - m).wait_send())
            return carry

        lax.fori_loop(0, ITERS, sent, 0)
        others(16, target, lambda a: cam_copy(a, slot).wait_send())

        @pl.when(gives_low)
        def _():
            others(16, low_target, lambda a: rim_copy(False, a, gz).wait_send())

        @pl.when(gives_high)
        def _():
            others(16, high_target, lambda a: rim_copy(True, a, gz).wait_send())


def per_device(sizes, camera, initial, psf_taps):
    held = pl.BlockSpec(memory_space=pl.ANY)
    dma = pltpu.SemaphoreType.DMA
    rows = initial.reshape(256, 128)
    result = pl.pallas_call(
        functools.partial(kernel, sizes),
        out_shape=jax.ShapeDtypeStruct((256, 128), F32),
        in_specs=[held, held, held],
        out_specs=pl.BlockSpec(memory_space=pltpu.VMEM),
        scratch_shapes=[
            pltpu.VMEM((VIEWS, 32, 4, 256), BF16),
            pltpu.VMEM((256, 128), F32),
            pltpu.VMEM((VIEWS, 3, TAPS), F32),
            dma((3,)),
            pltpu.VMEM((128, 256), F32),
            pltpu.VMEM((ITERS, 192, 9 * 256), BF16),
            pltpu.VMEM((VIEWS, 256, 256), BF16),
            pltpu.VMEM((VIEWS, 160, 256), F32),
            pltpu.VMEM((VIEWS, 384, 256), BF16),
            pltpu.VMEM((VIEWS, 9 * 256, 256), BF16),
            pltpu.VMEM((9, VIEWS * 256, 256), BF16),
            pltpu.VMEM((VIEWS, 160, 384), F32),
            pltpu.VMEM((VIEWS, 128, 256), F32),
            pltpu.VMEM((24, 128), F32),
            pltpu.VMEM((24, 128), F32),
            pltpu.VMEM((48 * 8, 128), F32),
            pltpu.VMEM((2, 48 * 8, 128), F32),
            pltpu.VMEM((48 * 8, 128), F32),
            pltpu.VMEM((2, 48 * 8, 128), F32),
            pltpu.VMEM((16, 128), F32),
            pltpu.VMEM((2, 96, 1024), BF16),
            pltpu.VMEM((4, 1024, 256), BF16),
            pltpu.VMEM((16, 3, 32, 128), BF16),
            pltpu.VMEM((16, 3, 32, 128), BF16),
            pltpu.VMEM((2, 4, 3, 16, 128), BF16),
            pltpu.VMEM((VIEWS, 160, 256), BF16),
            pltpu.VMEM((128, VIEWS * 256), BF16),
            pltpu.VMEM((2, 128, 256), F32),
            pltpu.VMEM((256, 128), F32),
            pltpu.VMEM((128, 256), F32),
            pltpu.VMEM((ITERS, 9, 144, 256), BF16),
            pltpu.VMEM((ITERS, 9, 144, 256), BF16),
            dma((16,)), dma((16,)),
            dma((2, 16)), dma((2, 4)),
            dma((ITERS, 27)), dma((ITERS, 27)),
            dma((ITERS, 9)), dma((ITERS, 9)),
        ],
        compiler_params=pltpu.CompilerParams(
            collective_id=0, has_side_effects=True, vmem_limit_bytes=56 * 1024 * 1024
        ),
    )(camera, rows, psf_taps)
    return result.reshape(initial.shape)


def solution(mesh):
    in_specs = (P(None, "gx", ("gy", "gz"), None), P("gx", "gy", "gz"), P())
    out_specs = P("gx", "gy", "gz")
    sizes = tuple(mesh.shape[a] for a in ("gx", "gy", "gz"))
    return jax.shard_map(
        functools.partial(per_device, sizes),
        mesh=mesh, in_specs=in_specs, out_specs=out_specs, check_vma=False,
    )
```

time: 225 us -> 75 us (0.33)
  the two profiles are of different devices: /device:TPU:312 before, /device:TPU:168 now
where the time goes in v2:
time: 75 us; the launch traced here: 74.8 us
  Pallas kernels  73.3 us (98%)
  local copies, waits for them, and re-layouts  1.57 us (2%)
    pallas_call x1, Pallas kernels, per_device(): pl.pallas_call(functools.partial(kernel, sizes), out_shape=jax.ShapeDtype...  73.3 us
    unnamed x1, local copies, waits for them, and re-layouts  1.57 us

profile of v2, /device:TPU:168, one launch (start us, length us, event | category | flops | bytes accessed | tf_op | source)
XLA Modules:
  0.0 74.8 jit_solution(14194838140295427908)
XLA Ops:
  0.0 73.3 %shard_map.37 = f32[256,128]{1,0:T(8,128)} custom-call(bf16[6,32,4,256]{3,2,1,0:T(4,128)(2,1)} %cam_hbm.1, f32[256,128]{1,0:T(8,128)} %bitcast.3, f32[6,3,31]{2,1,0:T(4,128)} %taps_hbm.1), custom_call_target="tpu_custom_call" | custom-call | tf_op jit(solution)/shard_map/pallas_call | solution.py:518
  73.3 1.6 %copy.5 = f32[16,16,128]{2,1,0:T(8,128)} copy(f32[16,16,128]{2,1,0:T(8,128)} %bitcast.2) | data formatting | bytes 262144

commit v3 on v2

--- a/solution.py
+++ b/solution.py
@@ -38,7 +38,7 @@
     cam_raw, init_ref, taps_ref, in_sem,
     est, ext, quot, inverse, ubuf, kf, kb, bzf, bzb, raw, back, xf, yf, xb, yb, scale,
     picked, place, cam_out, cam_in, rim_in, cam, third, part, flat, acc, code_out, code_in,
-    cam_send, cam_recv, rim_send, rim_recv, e_send, e_recv, c_send, c_recv,
+    cam_send, cam_recv, rim_send, rim_recv, e_send, e_recv, f_send, f_recv, c_send, c_recv,
 ):
     nx, ny, nz = sizes
     gx, gy, gz = lax.axis_index("gx"), lax.axis_index("gy"), lax.axis_index("gz")
@@ -52,25 +52,32 @@
     for copy in fetch:
         copy.start()
 
+    has_x = (gx > 0, True, gx < nx - 1)
+    has_y = (gy > 0, True, gy < ny - 1)
+    has_z = (below, True, above)
+
+    def steps(m):
+        return m % 9 // 3 - 1, m % 3 - 1, m // 9 - 1
+
     def place_of(m):
-        n = lax.rem(m, 9)
-        return gx + lax.div(n, 3) - 1, gy + lax.rem(n, 3) - 1, gz + lax.div(m, 9) - 1
+        dx, dy, dz = steps(m)
+        return gx + dx, gy + dy, gz + dz
 
     def there(m):
-        x, y, z = place_of(m)
-        return (x >= 0) & (x < nx) & (y >= 0) & (y < ny) & (z >= 0) & (z < nz)
-
-    def around(first, last, body):
-        def step(m, carry):
-            @pl.when(there(m) & (m != 13))
+        flags = [has[d + 1] for has, d in zip((has_x, has_y, has_z), steps(m)) if d]
+        return functools.reduce(jnp.logical_and, flags)
+
+    def around(ms, body):
+        for m in ms:
+            @pl.when(there(m))
             def _():
                 body(m)
 
-            return carry
-
-        lax.fori_loop(first, last, step, 0)
-
-    part_z, part_i = gx // 4, gx % 4
+    everyone = sorted((m for m in range(27) if m != 13), key=lambda m: -sum(map(abs, steps(m))))
+    rims = [m for m in everyone if m // 9 != 1]
+    sides = [m for m in everyone if m // 9 == 1]
+
+    part_z, part_i = gx >> 2, gx & 3
 
     def is_self(place):
         return (place[0] == gx) & (place[2] == gz)
@@ -97,15 +104,11 @@
         return a, gy, part_z - 1
 
     def others(count, place, body):
-        def step(s, carry):
+        for s in range(count):
             @pl.when(jnp.logical_not(is_self(place(s))))
             def _():
                 body(s)
 
-            return carry
-
-        lax.fori_loop(0, count, step, 0)
-
     barrier = pltpu.get_barrier_semaphore()
 
     def greet(place):
@@ -121,7 +124,7 @@
     def _():
         others(4, high_source, lambda k: greet(high_source(k)))
 
-    around(0, 27, lambda m: greet(place_of(m)))
+    around(everyone, lambda m: greet(place_of(m)))
 
     def one(flag):
         return flag.astype(jnp.int32)
@@ -134,26 +137,17 @@
     greetings += one(gives_high) * (16 - one(part_z - 1 == gz))
 
     with jax.named_scope("zeros"):
-        def clear(m, carry):
-            @pl.when(jnp.logical_not(there(m)))
-            def _():
-                lanes = pl.ds(pl.multiple_of(lax.rem(m, 9) * 256, 256), 256)
-                for it in range(ITERS):
-                    @pl.when(m < 9)
-                    def _():
-                        ext[it, 128:160, lanes] = jnp.zeros((32, 256), BF16)
-
-                    @pl.when((m >= 9) & (m < 18))
-                    def _():
-                        ext[it, 0:128, lanes] = jnp.zeros((128, 256), BF16)
-
-                    @pl.when(m >= 18)
-                    def _():
-                        ext[it, 160:192, lanes] = jnp.zeros((32, 256), BF16)
-
-            return carry
-
-        lax.fori_loop(0, 27, clear, 0)
+        for m in everyone:
+            step, lanes = m // 9, slice(m % 9 * 256, m % 9 * 256 + 256)
+            rows = (slice(128, 160), slice(0, 128), slice(160, 192))[step]
+
+            for it in range(ITERS):
+                sender = m if it or m in (4, 22) else 9 + m % 9
+
+                @pl.when(jnp.logical_not(there(sender)))
+                def _():
+                    ext[it, rows, lanes] = jnp.zeros((rows.stop - rows.start, 256), BF16)
+
         quot[:, 160:256, :] = jnp.zeros((VIEWS, 96, 256), BF16)
         place[...] = jnp.zeros(place.shape, BF16)
         raw[...] = jnp.zeros((24, 128), F32)
@@ -239,27 +233,37 @@
 
             others(16, high_target, lambda a: rim_copy(True, a, gz).start())
 
-    def e_copy(it, step, m, at):
-        first, count, to = ((0, 32, 160), (0, 128, 0), (96, 32, 128))[step + 1]
-        lanes = pl.ds(pl.multiple_of(lax.rem(at, 9) * 256, 256), 256)
+    def e_copy(it, m, at):
+        first, count, to = ((0, 32, 160), (0, 128, 0), (96, 32, 128))[m // 9]
         return pltpu.make_async_remote_copy(
             src_ref=ext.at[it, pl.ds(first, count), pl.ds(1024, 256)],
-            dst_ref=ext.at[it, pl.ds(to, count), lanes],
+            dst_ref=ext.at[it, pl.ds(to, count), pl.ds(at % 9 * 256, 256)],
             send_sem=e_send.at[it, m],
             recv_sem=e_recv.at[it, at],
             device_id=place_of(m),
             device_id_type=MESH,
         )
 
-    def each_estimate(act):
-        for step in (-1, 1, 0):
-            around(9 * (step + 1), 9 * (step + 2), lambda m: act(step, m))
-
-    def send_estimate(it):
-        each_estimate(lambda step, m: e_copy(it, step, m, 26 - m).start())
-
+    def forward_copy(m, at):
+        return pltpu.make_async_remote_copy(
+            src_ref=ext.at[0, pl.ds(128, 64), pl.ds(1024, 256)],
+            dst_ref=ext.at[0, pl.ds(128, 64), pl.ds(at % 9 * 256, 256)],
+            send_sem=f_send.at[m - 9],
+            recv_sem=f_recv.at[at - 9],
+            device_id=place_of(m),
+            device_id_type=MESH,
+        )
+
+    def send_estimate(it, ms):
+        around(ms, lambda m: e_copy(it, m, 26 - m).start())
+
+    def wait_estimate(it, ms):
+        around(ms, lambda m: e_copy(it, m, m).wait_recv())
+
+    vertical = (4, 22)
     with jax.named_scope("send estimate"):
-        send_estimate(0)
+        send_estimate(0, vertical)
+        send_estimate(0, sides)
 
     fetch[2].wait()
     with jax.named_scope("taps"):
@@ -305,6 +309,10 @@
 
         lax.fori_loop(0, 9 * VIEWS, products, 0)
 
+    with jax.named_scope("forward rims"):
+        wait_estimate(0, vertical)
+        around(sides, lambda m: forward_copy(m, 26 - m).start())
+
     with jax.named_scope("bands"):
         def bands(block, carry):
             r = iota((8, 128), 0) + block * 8
@@ -353,35 +361,6 @@
         scale[0:8, :] = jnp.broadcast_to(f_scale, (8, 128))
         scale[8:16, :] = jnp.broadcast_to(b_scale, (8, 128))
 
-    def factor(row):
-        value = scale[row : row + 1, :]
-        return jnp.concatenate([value, value], axis=1)
-
-    def blur(it):
-        for v in range(VIEWS):
-            u = dot(ext[it], kf[v])
-            high = u.astype(BF16)
-            ubuf[v, 0:192, :] = high
-            ubuf[v, 192:384, :] = (u - high.astype(F32)).astype(BF16)
-        for v in range(VIEWS):
-            inverse[v] = factor(v) / dot(bzf[v].astype(BF16), ubuf[v])
-
-    def wait_estimate(it):
-        each_estimate(lambda step, m: e_copy(it, step, m, m).wait_recv())
-
-    def quotients():
-        row = iota((32, 256), 0)
-        seen = jnp.where(row < 16, one(below), one(above)) > 0
-        for v in range(VIEWS):
-            quot[v, 0:128, :] = (cam[v, 0:128, :].astype(F32) * inverse[v, 0:128, :]).astype(BF16)
-            rim = jnp.where(seen, cam[v, 128:160, :].astype(F32) * inverse[v, 128:160, :], 0.0)
-            quot[v, 128:160, :] = rim.astype(BF16)
-
-    with jax.named_scope("wait estimate"):
-        wait_estimate(0)
-    with jax.named_scope("blur"):
-        blur(0)
-
     with jax.named_scope("back products"):
         def back_products(i, carry):
             v, n = i // 9, i % 9
@@ -397,6 +376,33 @@
 
         lax.fori_loop(0, 9 * VIEWS, back_products, 0)
 
+    def factor(row):
+        value = scale[row : row + 1, :]
+        return jnp.concatenate([value, value], axis=1)
+
+    def blur(it):
+        for v in range(VIEWS):
+            u = dot(ext[it], kf[v])
+            high = u.astype(BF16)
+            ubuf[v, 0:192, :] = high
+            ubuf[v, 192:384, :] = (u - high.astype(F32)).astype(BF16)
+        for v in range(VIEWS):
+            inverse[v] = factor(v) / dot(bzf[v].astype(BF16), ubuf[v])
+
+    def quotients():
+        row = iota((32, 256), 0)
+        seen = jnp.where(row < 16, one(below), one(above)) > 0
+        for v in range(VIEWS):
+            quot[v, 0:128, :] = (cam[v, 0:128, :].astype(F32) * inverse[v, 0:128, :]).astype(BF16)
+            rim = jnp.where(seen, cam[v, 128:160, :].astype(F32) * inverse[v, 128:160, :], 0.0)
+            quot[v, 128:160, :] = rim.astype(BF16)
+
+    with jax.named_scope("wait estimate"):
+        wait_estimate(0, sides)
+        around(sides, lambda m: forward_copy(m, m).wait_recv())
+    with jax.named_scope("blur"):
+        blur(0)
+
     with jax.named_scope("camera wait"):
         others(16, source, lambda s: cam_copy(0, s).wait_recv())
 
@@ -439,10 +445,28 @@
             device_id_type=MESH,
         )
 
+    def sent():
+        around(vertical, lambda m: e_copy(0, m, 26 - m).wait_send())
+        around(sides, lambda m: e_copy(0, m, 26 - m).wait_send())
+        around(sides, lambda m: forward_copy(m, 26 - m).wait_send())
+        for it in range(1, ITERS):
+            around(everyone, lambda m: e_copy(it, m, 26 - m).wait_send())
+        for it in range(ITERS - 1):
+            around(sides, lambda m: c_copy(it, m - 9, 17 - m).wait_send())
+        others(16, target, lambda a: cam_copy(a, slot).wait_send())
+
+        @pl.when(gives_low)
+        def _():
+            others(16, low_target, lambda a: rim_copy(False, a, gz).wait_send())
+
+        @pl.when(gives_high)
+        def _():
+            others(16, high_target, lambda a: rim_copy(True, a, gz).wait_send())
+
     for it in range(ITERS):
         if it > 0:
             with jax.named_scope("wait estimate 2"):
-                wait_estimate(it)
+                wait_estimate(it, everyone)
             with jax.named_scope("blur 2"):
                 blur(it)
         with jax.named_scope("quotients"):
@@ -454,7 +478,7 @@
 
         with jax.named_scope("partial sums"):
             for count, n in enumerate(ORDER):
-                @pl.when(there(jnp.int32(9 + n)))
+                @pl.when(there(9 + n))
                 def _():
                     with jax.named_scope("encode"):
                         work = part.at[count % 2]
@@ -471,9 +495,13 @@
         with jax.named_scope("own sum"):
             acc[...] = dot(third[...], kb[4])
 
+        if it == ITERS - 1:
+            with jax.named_scope("sent"):
+                sent()
+
         with jax.named_scope("collect"):
             for n in reversed(ORDER):
-                @pl.when(there(jnp.int32(9 + n)))
+                @pl.when(there(9 + n))
                 def _():
                     c_copy(it, n, n).wait_recv()
                     with jax.named_scope("add"):
@@ -486,29 +514,17 @@
         if it < ITERS - 1:
             ext[it + 1, 0:128, 1024:1280] = est[...].astype(BF16)
             with jax.named_scope("send estimate 2"):
-                send_estimate(it + 1)
+                send_estimate(it + 1, everyone)
 
     with jax.named_scope("layout out"):
         flat[...] = est[...].T
         for y in range(16):
             out_ref[pl.ds(y, 16, stride=16), :] = flat[y * 16 : (y + 1) * 16, :]
 
-    with jax.named_scope("sent"):
-        def sent(it, carry):
-            each_estimate(lambda step, m: e_copy(it, step, m, 26 - m).wait_send())
-            around(9, 18, lambda m: c_copy(it, m - 9, 17 - m).wait_send())
-            return carry
-
-        lax.fori_loop(0, ITERS, sent, 0)
-        others(16, target, lambda a: cam_copy(a, slot).wait_send())
-
-        @pl.when(gives_low)
-        def _():
-            others(16, low_target, lambda a: rim_copy(False, a, gz).wait_send())
-
-        @pl.when(gives_high)
-        def _():
-            others(16, high_target, lambda a: rim_copy(True, a, gz).wait_send())
+    for n in ORDER:
+        @pl.when(there(9 + n))
+        def _():
+            c_copy(ITERS - 1, n, 8 - n).wait_send()
 
 
 def per_device(sizes, camera, initial, psf_taps):
@@ -556,6 +572,7 @@
             dma((16,)), dma((16,)),
             dma((2, 16)), dma((2, 4)),
             dma((ITERS, 27)), dma((ITERS, 27)),
+            dma((9,)), dma((9,)),
             dma((ITERS, 9)), dma((ITERS, 9)),
         ],
         compiler_params=pltpu.CompilerParams(

time: 75 us -> 70.5 us (0.940)
  the two profiles are of different devices: /device:TPU:168 before, /device:TPU:120 now
where the time goes in v3:
time: 70.5 us; the launch traced here: 70.4 us
  Pallas kernels  68.8 us (98%)
  local copies, waits for them, and re-layouts  1.57 us (2%)
    pallas_call x1, Pallas kernels, per_device(): pl.pallas_call(functools.partial(kernel, sizes), out_shape=jax.ShapeDtype...  68.8 us
    unnamed x1, local copies, waits for them, and re-layouts  1.57 us

profile of v3, /device:TPU:120, one launch (start us, length us, event | category | flops | bytes accessed | tf_op | source)
XLA Modules:
  0.0 70.4 jit_solution(8269573764510581546)
XLA Ops:
  0.0 68.8 %shard_map.37 = f32[256,128]{1,0:T(8,128)} custom-call(bf16[6,32,4,256]{3,2,1,0:T(4,128)(2,1)} %cam_hbm.1, f32[256,128]{1,0:T(8,128)} %bitcast.3, f32[6,3,31]{2,1,0:T(4,128)} %taps_hbm.1), custom_call_target="tpu_custom_call" | custom-call | tf_op jit(solution)/shard_map/pallas_call | solution.py:534
  68.8 1.6 %copy.5 = f32[16,16,128]{2,1,0:T(8,128)} copy(f32[16,16,128]{2,1,0:T(8,128)} %bitcast.2) | data formatting | bytes 262144

commit v4 on v3

--- a/solution.py
+++ b/solution.py
@@ -37,9 +37,10 @@
     sizes, cam_hbm, init_hbm, taps_hbm, out_ref,
     cam_raw, init_ref, taps_ref, in_sem,
     est, ext, quot, inverse, ubuf, kf, kb, bzf, bzb, raw, back, xf, yf, xb, yb, scale,
-    picked, place, cam_out, cam_in, rim_in, cam, third, part, flat, acc, code_out, code_in,
-    cam_send, cam_recv, rim_send, rim_recv, e_send, e_recv, f_send, f_recv, c_send, c_recv,
+    picked, place, cam_out, cam_in, rim_in, cam, third, part, flat, acc, code_out0, code_out1, code_out2, code_in0, code_in1, code_in2,
+    cam_send, cam_recv, rim_send, rim_recv, e_send, e_recv, f_send, f_recv, c_send, c_recv, m_send, m_recv,
 ):
+    code_out, code_in = (code_out0, code_out1, code_out2), (code_in0, code_in1, code_in2)
     nx, ny, nz = sizes
     gx, gy, gz = lax.axis_index("gx"), lax.axis_index("gy"), lax.axis_index("gz")
     below, above = gz > 0, gz < nz - 1
@@ -94,8 +95,9 @@
     def target(a):
         return a, gy, part_z
 
-    gives_low = (part_i == 3) & (part_z < nz - 1)
-    gives_high = (part_i == 0) & (part_z > 0)
+    gives_low = (part_i == 3) & (part_z == 1)
+    gives_high = (part_i == 0) & (part_z == 2)
+    takes_low, takes_high = gz == 2, gz == 1
 
     def low_target(a):
         return a, gy, part_z + 1
@@ -116,11 +118,11 @@
 
     others(16, source, lambda s: greet(source(s)))
 
-    @pl.when(below)
+    @pl.when(takes_low)
     def _():
         others(4, low_source, lambda k: greet(low_source(k)))
 
-    @pl.when(above)
+    @pl.when(takes_high)
     def _():
         others(4, high_source, lambda k: greet(high_source(k)))
 
@@ -210,29 +212,6 @@
             device_id_type=MESH,
         )
 
-    with jax.named_scope("send camera"):
-        @pl.when(part_z == gz)
-        def _():
-            cam_in[slot] = cam_out[gx]
-
-        others(16, target, lambda a: cam_copy(a, slot).start())
-
-        @pl.when(gives_low)
-        def _():
-            @pl.when(part_z + 1 == gz)
-            def _():
-                rim_in[0, gz] = cam_out[gx, :, 16:32, :]
-
-            others(16, low_target, lambda a: rim_copy(False, a, gz).start())
-
-        @pl.when(gives_high)
-        def _():
-            @pl.when(part_z - 1 == gz)
-            def _():
-                rim_in[1, gz] = cam_out[gx, :, 0:16, :]
-
-            others(16, high_target, lambda a: rim_copy(True, a, gz).start())
-
     def e_copy(it, m, at):
         first, count, to = ((0, 32, 160), (0, 128, 0), (96, 32, 128))[m // 9]
         return pltpu.make_async_remote_copy(
@@ -261,8 +240,33 @@
         around(ms, lambda m: e_copy(it, m, m).wait_recv())
 
     vertical = (4, 22)
+    with jax.named_scope("send rims"):
+        send_estimate(0, vertical)
+
+    with jax.named_scope("send camera"):
+        @pl.when(part_z == gz)
+        def _():
+            cam_in[slot] = cam_out[gx]
+
+        others(16, target, lambda a: cam_copy(a, slot).start())
+
+        @pl.when(gives_low)
+        def _():
+            @pl.when(part_z + 1 == gz)
+            def _():
+                rim_in[0, gz] = cam_out[gx, :, 16:32, :]
+
+            others(16, low_target, lambda a: rim_copy(False, a, gz).start())
+
+        @pl.when(gives_high)
+        def _():
+            @pl.when(part_z - 1 == gz)
+            def _():
+                rim_in[1, gz] = cam_out[gx, :, 0:16, :]
+
+            others(16, high_target, lambda a: rim_copy(True, a, gz).start())
+
     with jax.named_scope("send estimate"):
-        send_estimate(0, vertical)
         send_estimate(0, sides)
 
     fetch[2].wait()
@@ -403,47 +407,118 @@
     with jax.named_scope("blur"):
         blur(0)
 
-    with jax.named_scope("camera wait"):
-        others(16, source, lambda s: cam_copy(0, s).wait_recv())
-
-        @pl.when(below)
-        def _():
-            others(4, low_source, lambda k: rim_copy(False, 0, k).wait_recv())
-
-        @pl.when(above)
-        def _():
-            others(4, high_source, lambda k: rim_copy(True, 0, k).wait_recv())
-
-    with jax.named_scope("assemble"):
-        def pair(r, even, odd):
-            low = iota(even.shape, 1) < 64
-            even, odd = even.astype(F32), odd.astype(F32)
-            if r == 0:
-                return jnp.where(low, even, odd).astype(BF16)
-            return pltpu.roll(jnp.where(low, odd, even), 64, 1).astype(BF16)
-
+    def mate_copy(first, to):
+        return pltpu.make_async_remote_copy(
+            src_ref=cam.at[:, pl.ds(first, 16), :],
+            dst_ref=cam.at[:, pl.ds(to, 16), :],
+            send_sem=m_send,
+            recv_sem=m_recv,
+            device_id=(gx, gy, gz ^ 1),
+            device_id_type=MESH,
+        )
+
+    def pair(r, even, odd):
+        low = iota(even.shape, 1) < 64
+        even, odd = even.astype(F32), odd.astype(F32)
+        if r == 0:
+            return jnp.where(low, even, odd).astype(BF16)
+        return pltpu.roll(jnp.where(low, odd, even), 64, 1).astype(BF16)
+
+    def assemble(z):
+        for k in range(4):
+            @pl.when(jnp.logical_not(is_self(source(4 * z + k))))
+            def _():
+                cam_copy(0, 4 * z + k).wait_recv()
         for v in range(VIEWS):
             r, w = v // 3, v % 3
             for t in range(2):
-                lanes = slice(t * 128, (t + 1) * 128)
-                for z in range(4):
-                    cam[v, z * 32 : (z + 1) * 32, lanes] = pair(
-                        r, cam_in[z * 4 + 2 * t, w], cam_in[z * 4 + 2 * t + 1, w]
-                    )
-                for high in range(2):
-                    cam[v, 128 + high * 16 : 144 + high * 16, lanes] = pair(
-                        r, rim_in[high, 2 * t, w], rim_in[high, 2 * t + 1, w]
-                    )
-
-    def c_copy(it, n, at):
+                cam[v, z * 32 : (z + 1) * 32, t * 128 : (t + 1) * 128] = pair(
+                    r, cam_in[z * 4 + 2 * t, w], cam_in[z * 4 + 2 * t + 1, w]
+                )
+
+    def assemble_rim(high):
+        place = high_source if high else low_source
+        others(4, place, lambda k: rim_copy(high, 0, k).wait_recv())
+        for v in range(VIEWS):
+            r, w = v // 3, v % 3
+            for t in range(2):
+                cam[v, 128 + high * 16 : 144 + high * 16, t * 128 : (t + 1) * 128] = pair(
+                    r, rim_in[high, 2 * t, w], rim_in[high, 2 * t + 1, w]
+                )
+
+    even = (gz & 1) == 0
+    with jax.named_scope("camera in"):
+        @pl.when(even)
+        def _():
+            assemble(3)
+            mate_copy(112, 128).start()
+            assemble(0)
+
+        @pl.when(jnp.logical_not(even))
+        def _():
+            assemble(0)
+            mate_copy(0, 144).start()
+            assemble(3)
+
+        assemble(1)
+        assemble(2)
+
+        @pl.when(takes_low)
+        def _():
+            assemble_rim(0)
+
+        @pl.when(takes_high)
+        def _():
+            assemble_rim(1)
+
+        @pl.when(even)
+        def _():
+            mate_copy(0, 144).wait_recv()
+
+        @pl.when(jnp.logical_not(even))
+        def _():
+            mate_copy(112, 128).wait_recv()
+
+    parts = ((0, 1, 6, 7), (2, 3, 4, 5), tuple(range(8)))
+
+    def c_copy(part_of, n, at):
         return pltpu.make_async_remote_copy(
-            src_ref=code_out.at[it, n],
-            dst_ref=code_in.at[it, at],
-            send_sem=c_send.at[it, n],
-            recv_sem=c_recv.at[it, at],
+            src_ref=code_out[part_of].at[n],
+            dst_ref=code_in[part_of].at[at],
+            send_sem=c_send.at[part_of, n],
+            recv_sem=c_recv.at[part_of, at],
             device_id=place_of(9 + n),
             device_id_type=MESH,
         )
+
+    def encode(work, part_of, n):
+        groups, out = parts[part_of], code_out[part_of]
+        base = [work[g * 16 + 8 : g * 16 + 9, :] for g in groups]
+        base = jnp.concatenate(base + [jnp.zeros((16 - len(groups), 256), F32)], axis=0).astype(BF16)
+        out[n, len(groups) * 16 : len(groups) * 16 + 16, :] = base
+        base = base.astype(F32)
+        for i, g in enumerate(groups):
+            out[n, i * 16 : (i + 1) * 16, :] = (work[g * 16 : (g + 1) * 16, :] - base[i : i + 1, :]).astype(BF16)
+
+    def collect(part_of):
+        groups, code = parts[part_of], code_in[part_of]
+        for n in reversed(ORDER):
+            @pl.when(there(9 + n))
+            def _():
+                c_copy(part_of, n, n).wait_recv()
+                with jax.named_scope("add"):
+                    base = code[n, len(groups) * 16 : len(groups) * 16 + 16, :].astype(F32)
+                    for i, g in enumerate(groups):
+                        rows = slice(g * 16, (g + 1) * 16)
+                        acc[rows, :] += code[n, i * 16 : (i + 1) * 16, :].astype(F32) + base[i : i + 1, :]
+
+    def update(part_of, it):
+        for g in parts[part_of]:
+            rows = slice(g * 16, (g + 1) * 16)
+            value = est[rows, :] * acc[rows, :] / VIEWS
+            est[rows, :] = value
+            if it < ITERS - 1:
+                ext[it + 1, rows, 1024:1280] = value.astype(BF16)
 
     def sent():
         around(vertical, lambda m: e_copy(0, m, 26 - m).wait_send())
@@ -451,8 +526,16 @@
         around(sides, lambda m: forward_copy(m, 26 - m).wait_send())
         for it in range(1, ITERS):
             around(everyone, lambda m: e_copy(it, m, 26 - m).wait_send())
-        for it in range(ITERS - 1):
-            around(sides, lambda m: c_copy(it, m - 9, 17 - m).wait_send())
+        for part_of in range(2):
+            around(sides, lambda m: c_copy(part_of, m - 9, 17 - m).wait_send())
+
+        @pl.when(even)
+        def _():
+            mate_copy(112, 128).wait_send()
+
+        @pl.when(jnp.logical_not(even))
+        def _():
+            mate_copy(0, 144).wait_send()
         others(16, target, lambda a: cam_copy(a, slot).wait_send())
 
         @pl.when(gives_low)
@@ -476,45 +559,40 @@
                 value = dot(bzb[v].astype(BF16), quot[v]) * factor(8 + v)
                 third[:, v * 256 : (v + 1) * 256] = value.astype(BF16)
 
+        last = it == ITERS - 1
         with jax.named_scope("partial sums"):
             for count, n in enumerate(ORDER):
                 @pl.when(there(9 + n))
                 def _():
-                    with jax.named_scope("encode"):
-                        work = part.at[count % 2]
-                        work[...] = dot(third[...], kb[n])
-                        base = jnp.concatenate([work[g * 16 + 8 : g * 16 + 9, :] for g in range(8)], axis=0)
-                        base = base.astype(BF16).astype(F32)
-                        rest = jnp.zeros((8, 256), F32)
-                        code_out[it, n, 128:144, :] = jnp.concatenate([base, rest], axis=0).astype(BF16)
-                        for g in range(8):
-                            rows = slice(g * 16, (g + 1) * 16)
-                            code_out[it, n, rows, :] = (work[rows, :] - base[g : g + 1, :]).astype(BF16)
-                    c_copy(it, n, 8 - n).start()
+                    work = part.at[count % 2]
+                    work[...] = dot(third[...], kb[n])
+                    if last:
+                        encode(work, 2, n)
+                        c_copy(2, n, 8 - n).start()
+                    else:
+                        encode(work, 0, n)
+                        c_copy(0, n, 8 - n).start()
+                        encode(work, 1, n)
+            if not last:
+                for n in ORDER:
+                    @pl.when(there(9 + n))
+                    def _():
+                        c_copy(1, n, 8 - n).start()
 
         with jax.named_scope("own sum"):
             acc[...] = dot(third[...], kb[4])
-
-        if it == ITERS - 1:
+        if last:
             with jax.named_scope("sent"):
                 sent()
-
-        with jax.named_scope("collect"):
-            for n in reversed(ORDER):
-                @pl.when(there(9 + n))
-                def _():
-                    c_copy(it, n, n).wait_recv()
-                    with jax.named_scope("add"):
-                        base = code_in[it, n, 128:144, :].astype(F32)
-                        for g in range(8):
-                            rows = slice(g * 16, (g + 1) * 16)
-                            acc[rows, :] += code_in[it, n, rows, :].astype(F32) + base[g : g + 1, :]
-
-        est[...] = est[...] * acc[...] / VIEWS
-        if it < ITERS - 1:
-            ext[it + 1, 0:128, 1024:1280] = est[...].astype(BF16)
-            with jax.named_scope("send estimate 2"):
-                send_estimate(it + 1, everyone)
+            collect(2)
+            update(2, it)
+        else:
+            collect(0)
+            update(0, it)
+            send_estimate(it + 1, rims)
+            collect(1)
+            update(1, it)
+            send_estimate(it + 1, sides)
 
     with jax.named_scope("layout out"):
         flat[...] = est[...].T
@@ -524,7 +602,7 @@
     for n in ORDER:
         @pl.when(there(9 + n))
         def _():
-            c_copy(ITERS - 1, n, 8 - n).wait_send()
+            c_copy(2, n, 8 - n).wait_send()
 
 
 def per_device(sizes, camera, initial, psf_taps):
@@ -567,13 +645,13 @@
             pltpu.VMEM((2, 128, 256), F32),
             pltpu.VMEM((256, 128), F32),
             pltpu.VMEM((128, 256), F32),
-            pltpu.VMEM((ITERS, 9, 144, 256), BF16),
-            pltpu.VMEM((ITERS, 9, 144, 256), BF16),
+            *[pltpu.VMEM((9, rows, 256), BF16) for rows in (80, 80, 144) * 2],
             dma((16,)), dma((16,)),
             dma((2, 16)), dma((2, 4)),
             dma((ITERS, 27)), dma((ITERS, 27)),
             dma((9,)), dma((9,)),
-            dma((ITERS, 9)), dma((ITERS, 9)),
+            dma((3, 9)), dma((3, 9)),
+            dma(()), dma(()),
         ],
         compiler_params=pltpu.CompilerParams(
             collective_id=0, has_side_effects=True, vmem_limit_bytes=56 * 1024 * 1024

time: 70.5 us -> 67.6 us (0.959)
  the two profiles are of different devices: /device:TPU:120 before, /device:TPU:208 now
where the time goes in v4:
time: 67.6 us; the launch traced here: 67.5 us
  Pallas kernels  65.9 us (97%)
  local copies, waits for them, and re-layouts  1.57 us (2%)
    pallas_call x1, Pallas kernels, per_device(): pl.pallas_call(functools.partial(kernel, sizes), out_shape=jax.ShapeDtype...  65.9 us
    unnamed x1, local copies, waits for them, and re-layouts  1.57 us

profile of v4, /device:TPU:208, one launch (start us, length us, event | category | flops | bytes accessed | tf_op | source)
XLA Modules:
  0.0 67.5 jit_solution(428891091091638964)
XLA Ops:
  0.0 65.9 %shard_map.37 = f32[256,128]{1,0:T(8,128)} custom-call(bf16[6,32,4,256]{3,2,1,0:T(4,128)(2,1)} %cam_hbm.1, f32[256,128]{1,0:T(8,128)} %bitcast.3, f32[6,3,31]{2,1,0:T(4,128)} %taps_hbm.1), custom_call_target="tpu_custom_call" | custom-call | tf_op jit(solution)/shard_map/pallas_call | solution.py:612
  65.9 1.6 %copy.5 = f32[16,16,128]{2,1,0:T(8,128)} copy(f32[16,16,128]{2,1,0:T(8,128)} %bitcast.2) | data formatting | bytes 262144

commit v5 on v4

--- a/solution.py
+++ b/solution.py
@@ -38,7 +38,7 @@
     cam_raw, init_ref, taps_ref, in_sem,
     est, ext, quot, inverse, ubuf, kf, kb, bzf, bzb, raw, back, xf, yf, xb, yb, scale,
     picked, place, cam_out, cam_in, rim_in, cam, third, part, flat, acc, code_out0, code_out1, code_out2, code_in0, code_in1, code_in2,
-    cam_send, cam_recv, rim_send, rim_recv, e_send, e_recv, f_send, f_recv, c_send, c_recv, m_send, m_recv,
+    cam_send, cam_recv, rim_send, rim_recv, e_send, e_recv, g_send, g_recv, c_send, c_recv, m_send, m_recv,
 ):
     code_out, code_in = (code_out0, code_out1, code_out2), (code_in0, code_in1, code_in2)
     nx, ny, nz = sizes
@@ -144,15 +144,14 @@
             rows = (slice(128, 160), slice(0, 128), slice(160, 192))[step]
 
             for it in range(ITERS):
-                sender = m if it or m in (4, 22) else 9 + m % 9
-
-                @pl.when(jnp.logical_not(there(sender)))
+                @pl.when(jnp.logical_not(there(m)))
                 def _():
                     ext[it, rows, lanes] = jnp.zeros((rows.stop - rows.start, 256), BF16)
 
         quot[:, 160:256, :] = jnp.zeros((VIEWS, 96, 256), BF16)
         place[...] = jnp.zeros(place.shape, BF16)
         raw[...] = jnp.zeros((24, 128), F32)
+        ubuf[:, 192:256, :] = jnp.zeros((VIEWS, 64, 512), BF16)
 
     with jax.named_scope("sort camera"):
         row, col = iota((32, 256), 0), iota((32, 256), 1)
@@ -179,12 +178,20 @@
                 cam_out[2 * p, w] = block[w * 32 : (w + 1) * 32, 0:128]
                 cam_out[2 * p + 1, w] = block[w * 32 : (w + 1) * 32, 128:256]
 
+    parts = ((0, 1, 6, 7), (2, 3, 4, 5), tuple(range(8)))
+
+    def keep(it, part_of):
+        for i, g in enumerate(parts[part_of]):
+            first = part_of * 64 + i * 16
+            ext[it, first : first + 16, 1024:1280] = est[g * 16 : (g + 1) * 16, :].astype(BF16)
+
     fetch[1].wait()
     with jax.named_scope("layout in"):
         for y in range(16):
             flat[y * 16 : (y + 1) * 16, :] = init_ref[pl.ds(y, 16, stride=16), :]
         est[...] = flat[...].T
-        ext[0, 0:128, 1024:1280] = est[...].astype(BF16)
+        for part_of in range(2):
+            keep(0, part_of)
 
     with jax.named_scope("entry wait"):
         pl.semaphore_wait(barrier, greetings)
@@ -213,7 +220,7 @@
         )
 
     def e_copy(it, m, at):
-        first, count, to = ((0, 32, 160), (0, 128, 0), (96, 32, 128))[m // 9]
+        first, count, to = ((0, 32, 160), (0, 64 if it else 128, 0), (32, 32, 128))[m // 9]
         return pltpu.make_async_remote_copy(
             src_ref=ext.at[it, pl.ds(first, count), pl.ds(1024, 256)],
             dst_ref=ext.at[it, pl.ds(to, count), pl.ds(at % 9 * 256, 256)],
@@ -223,12 +230,12 @@
             device_id_type=MESH,
         )
 
-    def forward_copy(m, at):
+    def middle_copy(m, at):
         return pltpu.make_async_remote_copy(
-            src_ref=ext.at[0, pl.ds(128, 64), pl.ds(1024, 256)],
-            dst_ref=ext.at[0, pl.ds(128, 64), pl.ds(at % 9 * 256, 256)],
-            send_sem=f_send.at[m - 9],
-            recv_sem=f_recv.at[at - 9],
+            src_ref=ext.at[1, pl.ds(64, 64), pl.ds(1024, 256)],
+            dst_ref=ext.at[1, pl.ds(64, 64), pl.ds(at % 9 * 256, 256)],
+            send_sem=g_send.at[m - 9],
+            recv_sem=g_recv.at[at - 9],
             device_id=place_of(m),
             device_id_type=MESH,
         )
@@ -239,9 +246,8 @@
     def wait_estimate(it, ms):
         around(ms, lambda m: e_copy(it, m, m).wait_recv())
 
-    vertical = (4, 22)
-    with jax.named_scope("send rims"):
-        send_estimate(0, vertical)
+    with jax.named_scope("send estimate"):
+        send_estimate(0, everyone)
 
     with jax.named_scope("send camera"):
         @pl.when(part_z == gz)
@@ -265,9 +271,6 @@
                 rim_in[1, gz] = cam_out[gx, :, 0:16, :]
 
             others(16, high_target, lambda a: rim_copy(True, a, gz).start())
-
-    with jax.named_scope("send estimate"):
-        send_estimate(0, sides)
 
     fetch[2].wait()
     with jax.named_scope("taps"):
@@ -313,23 +316,19 @@
 
         lax.fori_loop(0, 9 * VIEWS, products, 0)
 
-    with jax.named_scope("forward rims"):
-        wait_estimate(0, vertical)
-        around(sides, lambda m: forward_copy(m, 26 - m).start())
-
     with jax.named_scope("bands"):
         def bands(block, carry):
             r = iota((8, 128), 0) + block * 8
             z_out = jnp.where(r < 128, r, jnp.where(r < 144, r - 144, r - 16))
             rows = pl.ds(pl.multiple_of(block * 8, 8), 8)
-            for t in range(3):
-                lane = iota((8, 128), 1) + t * 128
-                lane = jnp.where(lane < 192, lane, lane - 192)
-                z_in = jnp.where(lane < 128, lane, jnp.where(lane < 160, lane - 160, lane - 32))
+            lane = iota((8, 128), 1)
+            near = jnp.where(lane < 32, lane, jnp.where(lane < 64, lane + 64, lane - 32))
+            far = jnp.where(lane < 32, lane - 32, jnp.where(lane < 64, lane + 96, 4096))
+            for half, z_in in enumerate((near, far)):
                 index = inside(z_out - z_in + HALF)
                 for v in range(VIEWS):
                     band_f = jnp.broadcast_to(raw[16 + v : 17 + v, :], (8, 128))
-                    bzf[v, rows, t * 128 : (t + 1) * 128] = pick(band_f, index)
+                    bzf[v, rows, half * 128 : (half + 1) * 128] = pick(band_f, index)
             return carry
 
         lax.fori_loop(0, 20, bands, 0)
@@ -388,10 +387,11 @@
         for v in range(VIEWS):
             u = dot(ext[it], kf[v])
             high = u.astype(BF16)
-            ubuf[v, 0:192, :] = high
-            ubuf[v, 192:384, :] = (u - high.astype(F32)).astype(BF16)
+            ubuf[v, 0:192, 0:256] = high
+            ubuf[v, 0:192, 256:512] = (u - high.astype(F32)).astype(BF16)
         for v in range(VIEWS):
-            inverse[v] = factor(v) / dot(bzf[v].astype(BF16), ubuf[v])
+            halves = dot(bzf[v].astype(BF16), ubuf[v])
+            inverse[v] = factor(v) / (halves[:, 0:256] + halves[:, 256:512])
 
     def quotients():
         row = iota((32, 256), 0)
@@ -402,8 +402,7 @@
             quot[v, 128:160, :] = rim.astype(BF16)
 
     with jax.named_scope("wait estimate"):
-        wait_estimate(0, sides)
-        around(sides, lambda m: forward_copy(m, m).wait_recv())
+        wait_estimate(0, everyone)
     with jax.named_scope("blur"):
         blur(0)
 
@@ -479,8 +478,6 @@
         def _():
             mate_copy(112, 128).wait_recv()
 
-    parts = ((0, 1, 6, 7), (2, 3, 4, 5), tuple(range(8)))
-
     def c_copy(part_of, n, at):
         return pltpu.make_async_remote_copy(
             src_ref=code_out[part_of].at[n],
@@ -512,20 +509,16 @@
                         rows = slice(g * 16, (g + 1) * 16)
                         acc[rows, :] += code[n, i * 16 : (i + 1) * 16, :].astype(F32) + base[i : i + 1, :]
 
-    def update(part_of, it):
+    def update(part_of):
         for g in parts[part_of]:
             rows = slice(g * 16, (g + 1) * 16)
-            value = est[rows, :] * acc[rows, :] / VIEWS
-            est[rows, :] = value
-            if it < ITERS - 1:
-                ext[it + 1, rows, 1024:1280] = value.astype(BF16)
+            est[rows, :] = est[rows, :] * acc[rows, :] / VIEWS
 
     def sent():
-        around(vertical, lambda m: e_copy(0, m, 26 - m).wait_send())
-        around(sides, lambda m: e_copy(0, m, 26 - m).wait_send())
-        around(sides, lambda m: forward_copy(m, 26 - m).wait_send())
+        around(everyone, lambda m: e_copy(0, m, 26 - m).wait_send())
         for it in range(1, ITERS):
             around(everyone, lambda m: e_copy(it, m, 26 - m).wait_send())
+            around(sides, lambda m: middle_copy(m, 26 - m).wait_send())
         for part_of in range(2):
             around(sides, lambda m: c_copy(part_of, m - 9, 17 - m).wait_send())
 
@@ -550,6 +543,7 @@
         if it > 0:
             with jax.named_scope("wait estimate 2"):
                 wait_estimate(it, everyone)
+                around(sides, lambda m: middle_copy(m, m).wait_recv())
             with jax.named_scope("blur 2"):
                 blur(it)
         with jax.named_scope("quotients"):
@@ -585,14 +579,16 @@
             with jax.named_scope("sent"):
                 sent()
             collect(2)
-            update(2, it)
+            update(2)
         else:
             collect(0)
-            update(0, it)
-            send_estimate(it + 1, rims)
+            update(0)
+            keep(it + 1, 0)
+            send_estimate(it + 1, everyone)
             collect(1)
-            update(1, it)
-            send_estimate(it + 1, sides)
+            update(1)
+            keep(it + 1, 1)
+            around(sides, lambda m: middle_copy(m, 26 - m).start())
 
     with jax.named_scope("layout out"):
         flat[...] = est[...].T
@@ -623,10 +619,10 @@
             pltpu.VMEM((ITERS, 192, 9 * 256), BF16),
             pltpu.VMEM((VIEWS, 256, 256), BF16),
             pltpu.VMEM((VIEWS, 160, 256), F32),
-            pltpu.VMEM((VIEWS, 384, 256), BF16),
+            pltpu.VMEM((VIEWS, 256, 512), BF16),
             pltpu.VMEM((VIEWS, 9 * 256, 256), BF16),
             pltpu.VMEM((9, VIEWS * 256, 256), BF16),
-            pltpu.VMEM((VIEWS, 160, 384), F32),
+            pltpu.VMEM((VIEWS, 160, 256), F32),
             pltpu.VMEM((VIEWS, 128, 256), F32),
             pltpu.VMEM((24, 128), F32),
             pltpu.VMEM((24, 128), F32),
@@ -654,7 +650,7 @@
             dma(()), dma(()),
         ],
         compiler_params=pltpu.CompilerParams(
-            collective_id=0, has_side_effects=True, vmem_limit_bytes=56 * 1024 * 1024
+            collective_id=0, has_side_effects=True, vmem_limit_bytes=55040 * 1024
         ),
     )(camera, rows, psf_taps)
     return result.reshape(initial.shape)

time: 67.6 us -> 64.2 us (0.950)
  the two profiles are of different devices: /device:TPU:208 before, /device:TPU:216 now
where the time goes in v5:
time: 64.2 us; the launch traced here: 64 us
  Pallas kernels  62.6 us (98%)
  local copies, waits for them, and re-layouts  1.36 us (2%)
    pallas_call x1, Pallas kernels, per_device(): pl.pallas_call(functools.partial(kernel, sizes), out_shape=jax.ShapeDtype...  62.6 us
    unnamed x3, local copies, waits for them, and re-layouts  1.36 us

profile of v5, /device:TPU:216, one launch (start us, length us, event | category | flops | bytes accessed | tf_op | source)
XLA Modules:
  0.0 64.0 jit_solution(13964415192964544222)
XLA Ops:
  0.0 0.0 copy-start
  0.0 0.7 %copy-done = f32[6,3,31]{2,1,0:T(4,128)S(1)} copy-done((f32[6,3,31]{2,1,0:T(4,128)S(1)}, f32[6,3,31]{2,1,0:T(4,128)}, u32[]{:S(2)}) %copy-start) | copy-done | bytes 2256
  0.7 62.6 %shard_map.37 = f32[256,128]{1,0:T(8,128)S(1)} custom-call(bf16[6,32,4,256]{3,2,1,0:T(4,128)(2,1)} %cam_hbm.1, f32[256,128]{1,0:T(8,128)} %bitcast.3, f32[6,3,31]{2,1,0:T(4,128)S(1)} %copy-done), custom_call_target="tpu_custom_call" | custom-call | tf_op jit(solution)/shard_map/pallas_call | solution.py:608
  63.3 0.7 %copy.5 = f32[16,16,128]{2,1,0:T(8,128)} copy(f32[16,16,128]{2,1,0:T(8,128)S(1)} %bitcast.2) | data formatting | bytes 262144
Async XLA Ops:
  0.0 0.7 %copy-start = (f32[6,3,31]{2,1,0:T(4,128)S(1)}, f32[6,3,31]{2,1,0:T(4,128)}, u32[]{:S(2)}) copy-start(f32[6,3,31]{2,1,0:T(4,128)} %taps_hbm.1) | copy-start | bytes 6700

commit v6 on v5

--- a/solution.py
+++ b/solution.py
@@ -38,7 +38,7 @@
     cam_raw, init_ref, taps_ref, in_sem,
     est, ext, quot, inverse, ubuf, kf, kb, bzf, bzb, raw, back, xf, yf, xb, yb, scale,
     picked, place, cam_out, cam_in, rim_in, cam, third, part, flat, acc, code_out0, code_out1, code_out2, code_in0, code_in1, code_in2,
-    cam_send, cam_recv, rim_send, rim_recv, e_send, e_recv, g_send, g_recv, c_send, c_recv, m_send, m_recv,
+    cam_send, cam_recv, rim_send, rim_recv, e_send, e_recv, f_send, f_recv, g_send, g_recv, c_send, c_recv, m_send, m_recv,
 ):
     code_out, code_in = (code_out0, code_out1, code_out2), (code_in0, code_in1, code_in2)
     nx, ny, nz = sizes
@@ -144,7 +144,9 @@
             rows = (slice(128, 160), slice(0, 128), slice(160, 192))[step]
 
             for it in range(ITERS):
-                @pl.when(jnp.logical_not(there(m)))
+                sender = m if it or m in (4, 22) else 9 + m % 9
+
+                @pl.when(jnp.logical_not(there(sender)))
                 def _():
                     ext[it, rows, lanes] = jnp.zeros((rows.stop - rows.start, 256), BF16)
 
@@ -240,14 +242,25 @@
             device_id_type=MESH,
         )
 
+    def forward_copy(m, at):
+        return pltpu.make_async_remote_copy(
+            src_ref=ext.at[0, pl.ds(128, 64), pl.ds(1024, 256)],
+            dst_ref=ext.at[0, pl.ds(128, 64), pl.ds(at % 9 * 256, 256)],
+            send_sem=f_send.at[m - 9],
+            recv_sem=f_recv.at[at - 9],
+            device_id=place_of(m),
+            device_id_type=MESH,
+        )
+
     def send_estimate(it, ms):
         around(ms, lambda m: e_copy(it, m, 26 - m).start())
 
     def wait_estimate(it, ms):
         around(ms, lambda m: e_copy(it, m, m).wait_recv())
 
-    with jax.named_scope("send estimate"):
-        send_estimate(0, everyone)
+    vertical = (4, 22)
+    with jax.named_scope("send rims"):
+        send_estimate(0, vertical)
 
     with jax.named_scope("send camera"):
         @pl.when(part_z == gz)
@@ -271,6 +284,9 @@
                 rim_in[1, gz] = cam_out[gx, :, 0:16, :]
 
             others(16, high_target, lambda a: rim_copy(True, a, gz).start())
+
+    with jax.named_scope("send estimate"):
+        send_estimate(0, sides)
 
     fetch[2].wait()
     with jax.named_scope("taps"):
@@ -316,6 +332,10 @@
 
         lax.fori_loop(0, 9 * VIEWS, products, 0)
 
+    with jax.named_scope("forward rims"):
+        wait_estimate(0, vertical)
+        around(sides, lambda m: forward_copy(m, 26 - m).start())
+
     with jax.named_scope("bands"):
         def bands(block, carry):
             r = iota((8, 128), 0) + block * 8
@@ -402,7 +422,8 @@
             quot[v, 128:160, :] = rim.astype(BF16)
 
     with jax.named_scope("wait estimate"):
-        wait_estimate(0, everyone)
+        wait_estimate(0, sides)
+        around(sides, lambda m: forward_copy(m, m).wait_recv())
     with jax.named_scope("blur"):
         blur(0)
 
@@ -515,7 +536,9 @@
             est[rows, :] = est[rows, :] * acc[rows, :] / VIEWS
 
     def sent():
-        around(everyone, lambda m: e_copy(0, m, 26 - m).wait_send())
+        around(vertical, lambda m: e_copy(0, m, 26 - m).wait_send())
+        around(sides, lambda m: e_copy(0, m, 26 - m).wait_send())
+        around(sides, lambda m: forward_copy(m, 26 - m).wait_send())
         for it in range(1, ITERS):
             around(everyone, lambda m: e_copy(it, m, 26 - m).wait_send())
             around(sides, lambda m: middle_copy(m, 26 - m).wait_send())
@@ -646,6 +669,7 @@
             dma((2, 16)), dma((2, 4)),
             dma((ITERS, 27)), dma((ITERS, 27)),
             dma((9,)), dma((9,)),
+            dma((9,)), dma((9,)),
             dma((3, 9)), dma((3, 9)),
             dma(()), dma(()),
         ],

time: 64.2 us -> 65.8 us (1.025)
  the two profiles are of different devices: /device:TPU:216 before, /device:TPU:217 now
where the time goes in v6:
time: 65.8 us; the launch traced here: 65.6 us
  Pallas kernels  64.3 us (98%)
  local copies, waits for them, and re-layouts  1.36 us (2%)
    pallas_call x1, Pallas kernels, per_device(): pl.pallas_call(functools.partial(kernel, sizes), out_shape=jax.ShapeDtype...  64.3 us
    unnamed x3, local copies, waits for them, and re-layouts  1.36 us

profile of v6, /device:TPU:217, one launch (start us, length us, event | category | flops | bytes accessed | tf_op | source)
XLA Modules:
  0.0 65.6 jit_solution(11772049157150314063)
XLA Ops:
  0.0 0.0 copy-start
  0.0 0.7 %copy-done = f32[6,3,31]{2,1,0:T(4,128)S(1)} copy-done((f32[6,3,31]{2,1,0:T(4,128)S(1)}, f32[6,3,31]{2,1,0:T(4,128)}, u32[]{:S(2)}) %copy-start) | copy-done | bytes 2256
  0.7 64.3 %shard_map.37 = f32[256,128]{1,0:T(8,128)S(1)} custom-call(bf16[6,32,4,256]{3,2,1,0:T(4,128)(2,1)} %cam_hbm.1, f32[256,128]{1,0:T(8,128)} %bitcast.3, f32[6,3,31]{2,1,0:T(4,128)S(1)} %copy-done), custom_call_target="tpu_custom_call" | custom-call | tf_op jit(solution)/shard_map/pallas_call | solution.py:631
  65.0 0.7 %copy.5 = f32[16,16,128]{2,1,0:T(8,128)} copy(f32[16,16,128]{2,1,0:T(8,128)S(1)} %bitcast.2) | data formatting | bytes 262144
Async XLA Ops:
  0.0 0.7 %copy-start = (f32[6,3,31]{2,1,0:T(4,128)S(1)}, f32[6,3,31]{2,1,0:T(4,128)}, u32[]{:S(2)}) copy-start(f32[6,3,31]{2,1,0:T(4,128)} %taps_hbm.1) | copy-start | bytes 6700

commit v7 on v5

--- a/solution.py
+++ b/solution.py
@@ -37,7 +37,7 @@
     sizes, cam_hbm, init_hbm, taps_hbm, out_ref,
     cam_raw, init_ref, taps_ref, in_sem,
     est, ext, quot, inverse, ubuf, kf, kb, bzf, bzb, raw, back, xf, yf, xb, yb, scale,
-    picked, place, cam_out, cam_in, rim_in, cam, third, part, flat, acc, code_out0, code_out1, code_out2, code_in0, code_in1, code_in2,
+    picked, place, cam_out, cam_in, rim_in, cam, third, part, flat, acc, early, bases, code_out0, code_out1, code_out2, code_in0, code_in1, code_in2,
     cam_send, cam_recv, rim_send, rim_recv, e_send, e_recv, g_send, g_recv, c_send, c_recv, m_send, m_recv,
 ):
     code_out, code_in = (code_out0, code_out1, code_out2), (code_in0, code_in1, code_in2)
@@ -166,7 +166,7 @@
     fetch[0].wait()
     with jax.named_scope("sort camera 2"):
         for v in range(VIEWS):
-            r, w = v // 3, v % 3
+            r, w = v % 2, v // 2
             for y in range(4):
                 plane = cam_raw[v, :, y, :]
                 lanes = slice((r * 4 + y) * 128, (r * 4 + y + 1) * 128)
@@ -198,23 +198,25 @@
 
     slot = part_i * 4 + gz
 
-    def cam_copy(a, s):
+    pieces, views = (pl.ds(0, 2), pl.ds(2, 1)), (range(0, 4), range(4, 6))
+
+    def cam_copy(piece, a, s):
         return pltpu.make_async_remote_copy(
-            src_ref=cam_out.at[a],
-            dst_ref=cam_in.at[s],
-            send_sem=cam_send.at[a],
-            recv_sem=cam_recv.at[s],
+            src_ref=cam_out.at[a, pieces[piece]],
+            dst_ref=cam_in.at[s, pieces[piece]],
+            send_sem=cam_send.at[piece, a],
+            recv_sem=cam_recv.at[piece, s],
             device_id=target(a),
             device_id_type=MESH,
         )
 
-    def rim_copy(high, a, k):
+    def rim_copy(piece, high, a, k):
         first = 0 if high else 16
         return pltpu.make_async_remote_copy(
-            src_ref=cam_out.at[a, :, pl.ds(first, 16), :],
-            dst_ref=rim_in.at[int(high), k],
-            send_sem=rim_send.at[int(high), a],
-            recv_sem=rim_recv.at[int(high), k],
+            src_ref=cam_out.at[a, pieces[piece], pl.ds(first, 16), :],
+            dst_ref=rim_in.at[int(high), k, pieces[piece]],
+            send_sem=rim_send.at[piece, int(high), a],
+            recv_sem=rim_recv.at[piece, int(high), k],
             device_id=high_target(a) if high else low_target(a),
             device_id_type=MESH,
         )
@@ -254,23 +256,24 @@
         def _():
             cam_in[slot] = cam_out[gx]
 
-        others(16, target, lambda a: cam_copy(a, slot).start())
-
-        @pl.when(gives_low)
-        def _():
-            @pl.when(part_z + 1 == gz)
-            def _():
-                rim_in[0, gz] = cam_out[gx, :, 16:32, :]
-
-            others(16, low_target, lambda a: rim_copy(False, a, gz).start())
-
-        @pl.when(gives_high)
-        def _():
-            @pl.when(part_z - 1 == gz)
-            def _():
-                rim_in[1, gz] = cam_out[gx, :, 0:16, :]
-
-            others(16, high_target, lambda a: rim_copy(True, a, gz).start())
+        for piece in range(2):
+            others(16, target, lambda a: cam_copy(piece, a, slot).start())
+
+            @pl.when(gives_low)
+            def _():
+                others(16, low_target, lambda a: rim_copy(piece, False, a, gz).start())
+
+            @pl.when(gives_high)
+            def _():
+                others(16, high_target, lambda a: rim_copy(piece, True, a, gz).start())
+
+        @pl.when(gives_low & (part_z + 1 == gz))
+        def _():
+            rim_in[0, gz] = cam_out[gx, :, 16:32, :]
+
+        @pl.when(gives_high & (part_z - 1 == gz))
+        def _():
+            rim_in[1, gz] = cam_out[gx, :, 0:16, :]
 
     fetch[2].wait()
     with jax.named_scope("taps"):
@@ -393,10 +396,10 @@
             halves = dot(bzf[v].astype(BF16), ubuf[v])
             inverse[v] = factor(v) / (halves[:, 0:256] + halves[:, 256:512])
 
-    def quotients():
+    def quotients(some):
         row = iota((32, 256), 0)
         seen = jnp.where(row < 16, one(below), one(above)) > 0
-        for v in range(VIEWS):
+        for v in some:
             quot[v, 0:128, :] = (cam[v, 0:128, :].astype(F32) * inverse[v, 0:128, :]).astype(BF16)
             rim = jnp.where(seen, cam[v, 128:160, :].astype(F32) * inverse[v, 128:160, :], 0.0)
             quot[v, 128:160, :] = rim.astype(BF16)
@@ -406,12 +409,13 @@
     with jax.named_scope("blur"):
         blur(0)
 
-    def mate_copy(first, to):
+    def mate_copy(piece, first, to):
+        some = pl.ds(views[piece].start, len(views[piece]))
         return pltpu.make_async_remote_copy(
-            src_ref=cam.at[:, pl.ds(first, 16), :],
-            dst_ref=cam.at[:, pl.ds(to, 16), :],
-            send_sem=m_send,
-            recv_sem=m_recv,
+            src_ref=cam.at[some, pl.ds(first, 16), :],
+            dst_ref=cam.at[some, pl.ds(to, 16), :],
+            send_sem=m_send.at[piece],
+            recv_sem=m_recv.at[piece],
             device_id=(gx, gy, gz ^ 1),
             device_id_type=MESH,
         )
@@ -423,60 +427,61 @@
             return jnp.where(low, even, odd).astype(BF16)
         return pltpu.roll(jnp.where(low, odd, even), 64, 1).astype(BF16)
 
-    def assemble(z):
+    def assemble(piece, z):
         for k in range(4):
             @pl.when(jnp.logical_not(is_self(source(4 * z + k))))
             def _():
-                cam_copy(0, 4 * z + k).wait_recv()
-        for v in range(VIEWS):
-            r, w = v // 3, v % 3
+                cam_copy(piece, 0, 4 * z + k).wait_recv()
+        for v in views[piece]:
+            r, w = v % 2, v // 2
             for t in range(2):
                 cam[v, z * 32 : (z + 1) * 32, t * 128 : (t + 1) * 128] = pair(
                     r, cam_in[z * 4 + 2 * t, w], cam_in[z * 4 + 2 * t + 1, w]
                 )
 
-    def assemble_rim(high):
+    def assemble_rim(piece, high):
         place = high_source if high else low_source
-        others(4, place, lambda k: rim_copy(high, 0, k).wait_recv())
-        for v in range(VIEWS):
-            r, w = v // 3, v % 3
+        others(4, place, lambda k: rim_copy(piece, high, 0, k).wait_recv())
+        for v in views[piece]:
+            r, w = v % 2, v // 2
             for t in range(2):
                 cam[v, 128 + high * 16 : 144 + high * 16, t * 128 : (t + 1) * 128] = pair(
                     r, rim_in[high, 2 * t, w], rim_in[high, 2 * t + 1, w]
                 )
 
     even = (gz & 1) == 0
-    with jax.named_scope("camera in"):
+
+    def receive_camera(piece):
         @pl.when(even)
         def _():
-            assemble(3)
-            mate_copy(112, 128).start()
-            assemble(0)
+            assemble(piece, 3)
+            mate_copy(piece, 112, 128).start()
+            assemble(piece, 0)
 
         @pl.when(jnp.logical_not(even))
         def _():
-            assemble(0)
-            mate_copy(0, 144).start()
-            assemble(3)
-
-        assemble(1)
-        assemble(2)
+            assemble(piece, 0)
+            mate_copy(piece, 0, 144).start()
+            assemble(piece, 3)
+
+        assemble(piece, 1)
+        assemble(piece, 2)
 
         @pl.when(takes_low)
         def _():
-            assemble_rim(0)
+            assemble_rim(piece, 0)
 
         @pl.when(takes_high)
         def _():
-            assemble_rim(1)
+            assemble_rim(piece, 1)
 
         @pl.when(even)
         def _():
-            mate_copy(0, 144).wait_recv()
+            mate_copy(piece, 0, 144).wait_recv()
 
         @pl.when(jnp.logical_not(even))
         def _():
-            mate_copy(112, 128).wait_recv()
+            mate_copy(piece, 112, 128).wait_recv()
 
     def c_copy(part_of, n, at):
         return pltpu.make_async_remote_copy(
@@ -490,12 +495,14 @@
 
     def encode(work, part_of, n):
         groups, out = parts[part_of], code_out[part_of]
-        base = [work[g * 16 + 8 : g * 16 + 9, :] for g in groups]
-        base = jnp.concatenate(base + [jnp.zeros((16 - len(groups), 256), F32)], axis=0).astype(BF16)
-        out[n, len(groups) * 16 : len(groups) * 16 + 16, :] = base
-        base = base.astype(F32)
+        if part_of != 1:
+            base = jnp.concatenate(
+                [work[g * 16 + 8 : g * 16 + 9, :] for g in range(8)] + [jnp.zeros((8, 256), F32)], axis=0
+            ).astype(BF16)
+            out[n, len(groups) * 16 : len(groups) * 16 + 16, :] = base
+            bases[...] = base.astype(F32)
         for i, g in enumerate(groups):
-            out[n, i * 16 : (i + 1) * 16, :] = (work[g * 16 : (g + 1) * 16, :] - base[i : i + 1, :]).astype(BF16)
+            out[n, i * 16 : (i + 1) * 16, :] = (work[g * 16 : (g + 1) * 16, :] - bases[g : g + 1, :]).astype(BF16)
 
     def collect(part_of):
         groups, code = parts[part_of], code_in[part_of]
@@ -504,10 +511,13 @@
             def _():
                 c_copy(part_of, n, n).wait_recv()
                 with jax.named_scope("add"):
-                    base = code[n, len(groups) * 16 : len(groups) * 16 + 16, :].astype(F32)
+                    if part_of == 2:
+                        base = code[n, 128:144, :].astype(F32)
+                    else:
+                        base = code_in[0][n, 64:80, :].astype(F32)
                     for i, g in enumerate(groups):
                         rows = slice(g * 16, (g + 1) * 16)
-                        acc[rows, :] += code[n, i * 16 : (i + 1) * 16, :].astype(F32) + base[i : i + 1, :]
+                        acc[rows, :] += code[n, i * 16 : (i + 1) * 16, :].astype(F32) + base[g : g + 1, :]
 
     def update(part_of):
         for g in parts[part_of]:
@@ -522,22 +532,24 @@
         for part_of in range(2):
             around(sides, lambda m: c_copy(part_of, m - 9, 17 - m).wait_send())
 
-        @pl.when(even)
-        def _():
-            mate_copy(112, 128).wait_send()
-
-        @pl.when(jnp.logical_not(even))
-        def _():
-            mate_copy(0, 144).wait_send()
-        others(16, target, lambda a: cam_copy(a, slot).wait_send())
-
-        @pl.when(gives_low)
-        def _():
-            others(16, low_target, lambda a: rim_copy(False, a, gz).wait_send())
-
-        @pl.when(gives_high)
-        def _():
-            others(16, high_target, lambda a: rim_copy(True, a, gz).wait_send())
+        for piece in range(2):
+            @pl.when(even)
+            def _():
+                mate_copy(piece, 112, 128).wait_send()
+
+            @pl.when(jnp.logical_not(even))
+            def _():
+                mate_copy(piece, 0, 144).wait_send()
+
+            others(16, target, lambda a: cam_copy(piece, a, slot).wait_send())
+
+            @pl.when(gives_low)
+            def _():
+                others(16, low_target, lambda a: rim_copy(piece, False, a, gz).wait_send())
+
+            @pl.when(gives_high)
+            def _():
+                others(16, high_target, lambda a: rim_copy(piece, True, a, gz).wait_send())
 
     for it in range(ITERS):
         if it > 0:
@@ -546,12 +558,23 @@
                 around(sides, lambda m: middle_copy(m, m).wait_recv())
             with jax.named_scope("blur 2"):
                 blur(it)
-        with jax.named_scope("quotients"):
-            quotients()
-        with jax.named_scope("third"):
-            for v in range(VIEWS):
-                value = dot(bzb[v].astype(BF16), quot[v]) * factor(8 + v)
-                third[:, v * 256 : (v + 1) * 256] = value.astype(BF16)
+        for piece in range(2):
+            if it == 0:
+                receive_camera(piece)
+            with jax.named_scope("quotients"):
+                quotients(views[piece])
+            with jax.named_scope("third"):
+                for v in views[piece]:
+                    value = dot(bzb[v].astype(BF16), quot[v]) * factor(8 + v)
+                    third[:, v * 256 : (v + 1) * 256] = value.astype(BF16)
+            if it == 0 and piece == 0:
+                for n in range(9):
+                    early[n] = dot(third[:, 0:1024], kb[n, 0:1024, :])
+
+        def sums(n):
+            if it == 0:
+                return early[n] + dot(third[:, 1024:1536], kb[n, 1024:1536, :])
+            return dot(third[...], kb[n])
 
         last = it == ITERS - 1
         with jax.named_scope("partial sums"):
@@ -559,7 +582,7 @@
                 @pl.when(there(9 + n))
                 def _():
                     work = part.at[count % 2]
-                    work[...] = dot(third[...], kb[n])
+                    work[...] = sums(n)
                     if last:
                         encode(work, 2, n)
                         c_copy(2, n, 8 - n).start()
@@ -574,7 +597,7 @@
                         c_copy(1, n, 8 - n).start()
 
         with jax.named_scope("own sum"):
-            acc[...] = dot(third[...], kb[4])
+            acc[...] = sums(4)
         if last:
             with jax.named_scope("sent"):
                 sent()
@@ -641,13 +664,15 @@
             pltpu.VMEM((2, 128, 256), F32),
             pltpu.VMEM((256, 128), F32),
             pltpu.VMEM((128, 256), F32),
-            *[pltpu.VMEM((9, rows, 256), BF16) for rows in (80, 80, 144) * 2],
-            dma((16,)), dma((16,)),
-            dma((2, 16)), dma((2, 4)),
+            pltpu.VMEM((9, 128, 256), F32),
+            pltpu.VMEM((16, 256), F32),
+            *[pltpu.VMEM((9, rows, 256), BF16) for rows in (80, 64, 144) * 2],
+            dma((2, 16)), dma((2, 16)),
+            dma((2, 2, 16)), dma((2, 2, 4)),
             dma((ITERS, 27)), dma((ITERS, 27)),
             dma((9,)), dma((9,)),
             dma((3, 9)), dma((3, 9)),
-            dma(()), dma(()),
+            dma((2,)), dma((2,)),
         ],
         compiler_params=pltpu.CompilerParams(
             collective_id=0, has_side_effects=True, vmem_limit_bytes=55040 * 1024

time: 64.2 us -> 66.7 us (1.039)
  Pallas kernels: 62.6 us -> 65.1 us
    pallas_call x1, Pallas kernels: 62.6 us -> 65.1 us  [per_device(): pl.pallas_call(functools.partial(kernel, sizes), out_shape=jax.ShapeDtype...]
where the time goes in v7:
time: 66.7 us; the launch traced here: 66.5 us
  Pallas kernels  65.1 us (98%)
  local copies, waits for them, and re-layouts  1.36 us (2%)
    pallas_call x1, Pallas kernels, per_device(): pl.pallas_call(functools.partial(kernel, sizes), out_shape=jax.ShapeDtype...  65.1 us
    unnamed x3, local copies, waits for them, and re-layouts  1.36 us

profile of v7, /device:TPU:216, one launch (start us, length us, event | category | flops | bytes accessed | tf_op | source)
XLA Modules:
  0.0 66.5 jit_solution(13808887303757172331)
XLA Ops:
  0.0 0.0 copy-start
  0.0 0.7 %copy-done = f32[6,3,31]{2,1,0:T(4,128)S(1)} copy-done((f32[6,3,31]{2,1,0:T(4,128)S(1)}, f32[6,3,31]{2,1,0:T(4,128)}, u32[]{:S(2)}) %copy-start) | copy-done | bytes 2256
  0.7 65.1 %shard_map.37 = f32[256,128]{1,0:T(8,128)S(1)} custom-call(bf16[6,32,4,256]{3,2,1,0:T(4,128)(2,1)} %cam_hbm.1, f32[256,128]{1,0:T(8,128)} %bitcast.3, f32[6,3,31]{2,1,0:T(4,128)S(1)} %copy-done), custom_call_target="tpu_custom_call" | custom-call | tf_op jit(solution)/shard_map/pallas_call | solution.py:631
  65.9 0.7 copy.5
Async XLA Ops:
  0.0 0.7 %copy-start = (f32[6,3,31]{2,1,0:T(4,128)S(1)}, f32[6,3,31]{2,1,0:T(4,128)}, u32[]{:S(2)}) copy-start(f32[6,3,31]{2,1,0:T(4,128)} %taps_hbm.1) | copy-start | bytes 6700

commit v8 on v5

--- a/solution.py
+++ b/solution.py
@@ -37,8 +37,8 @@
     sizes, cam_hbm, init_hbm, taps_hbm, out_ref,
     cam_raw, init_ref, taps_ref, in_sem,
     est, ext, quot, inverse, ubuf, kf, kb, bzf, bzb, raw, back, xf, yf, xb, yb, scale,
-    picked, place, cam_out, cam_in, rim_in, cam, third, part, flat, acc, code_out0, code_out1, code_out2, code_in0, code_in1, code_in2,
-    cam_send, cam_recv, rim_send, rim_recv, e_send, e_recv, g_send, g_recv, c_send, c_recv, m_send, m_recv,
+    picked, place, cam_out, cam_in, rim_in, cam, third, part, flat, acc, bases, code_out0, code_out1, code_out2, code_in0, code_in1, code_in2,
+    cam_send, cam_recv, rim_send, rim_recv, e_send, e_recv, g_send, g_recv, c_send, c_recv, m_send, m_recv, r_send, r_recv,
 ):
     code_out, code_in = (code_out0, code_out1, code_out2), (code_in0, code_in1, code_in2)
     nx, ny, nz = sizes
@@ -55,7 +55,9 @@
 
     has_x = (gx > 0, True, gx < nx - 1)
     has_y = (gy > 0, True, gy < ny - 1)
-    has_z = (below, True, above)
+    has_z = (gz == 2, True, gz == 1)
+    even = (gz & 1) == 0
+    mate = (gx, gy, gz ^ 1)
 
     def steps(m):
         return m % 9 // 3 - 1, m % 3 - 1, m // 9 - 1
@@ -127,14 +129,15 @@
         others(4, high_source, lambda k: greet(high_source(k)))
 
     around(everyone, lambda m: greet(place_of(m)))
+    greet(mate)
 
     def one(flag):
         return flag.astype(jnp.int32)
 
     wide = 1 + one(gx > 0) + one(gx < nx - 1)
     tall = 1 + one(gy > 0) + one(gy < ny - 1)
-    deep = 1 + one(below) + one(above)
-    greetings = wide * tall * deep - 1 + 16 - one(part_z == gz)
+    deep = 1 + one(gz == 1) + one(gz == 2)
+    greetings = wide * tall * deep + 16 - one(part_z == gz)
     greetings += one(gives_low) * (16 - one(part_z + 1 == gz))
     greetings += one(gives_high) * (16 - one(part_z - 1 == gz))
 
@@ -143,8 +146,13 @@
             step, lanes = m // 9, slice(m % 9 * 256, m % 9 * 256 + 256)
             rows = (slice(128, 160), slice(0, 128), slice(160, 192))[step]
 
+            none = jnp.logical_not(there(m))
+            if step == 0:
+                none = none & even
+            elif step == 2:
+                none = none & jnp.logical_not(even)
             for it in range(ITERS):
-                @pl.when(jnp.logical_not(there(m)))
+                @pl.when(none)
                 def _():
                     ext[it, rows, lanes] = jnp.zeros((rows.stop - rows.start, 256), BF16)
 
@@ -240,6 +248,26 @@
             device_id_type=MESH,
         )
 
+    def mate_rims(it, up):
+        first, to = (32, 128) if up else (0, 160)
+        return pltpu.make_async_remote_copy(
+            src_ref=ext.at[it, pl.ds(first, 32), :],
+            dst_ref=ext.at[it, pl.ds(to, 32), :],
+            send_sem=r_send.at[it],
+            recv_sem=r_recv.at[it],
+            device_id=mate,
+            device_id_type=MESH,
+        )
+
+    def with_mate(body):
+        @pl.when(even)
+        def _():
+            body(True)
+
+        @pl.when(jnp.logical_not(even))
+        def _():
+            body(False)
+
     def send_estimate(it, ms):
         around(ms, lambda m: e_copy(it, m, 26 - m).start())
 
@@ -316,6 +344,10 @@
 
         lax.fori_loop(0, 9 * VIEWS, products, 0)
 
+    with jax.named_scope("pass rims"):
+        wait_estimate(0, sides)
+        with_mate(lambda up: mate_rims(0, up).start())
+
     with jax.named_scope("bands"):
         def bands(block, carry):
             r = iota((8, 128), 0) + block * 8
@@ -402,7 +434,8 @@
             quot[v, 128:160, :] = rim.astype(BF16)
 
     with jax.named_scope("wait estimate"):
-        wait_estimate(0, everyone)
+        wait_estimate(0, rims)
+        with_mate(lambda up: mate_rims(0, not up).wait_recv())
     with jax.named_scope("blur"):
         blur(0)
 
@@ -412,7 +445,7 @@
             dst_ref=cam.at[:, pl.ds(to, 16), :],
             send_sem=m_send,
             recv_sem=m_recv,
-            device_id=(gx, gy, gz ^ 1),
+            device_id=mate,
             device_id_type=MESH,
         )
 
@@ -445,7 +478,6 @@
                     r, rim_in[high, 2 * t, w], rim_in[high, 2 * t + 1, w]
                 )
 
-    even = (gz & 1) == 0
     with jax.named_scope("camera in"):
         @pl.when(even)
         def _():
@@ -490,12 +522,14 @@
 
     def encode(work, part_of, n):
         groups, out = parts[part_of], code_out[part_of]
-        base = [work[g * 16 + 8 : g * 16 + 9, :] for g in groups]
-        base = jnp.concatenate(base + [jnp.zeros((16 - len(groups), 256), F32)], axis=0).astype(BF16)
-        out[n, len(groups) * 16 : len(groups) * 16 + 16, :] = base
-        base = base.astype(F32)
+        if part_of != 1:
+            base = jnp.concatenate(
+                [work[g * 16 + 8 : g * 16 + 9, :] for g in range(8)] + [jnp.zeros((8, 256), F32)], axis=0
+            ).astype(BF16)
+            out[n, len(groups) * 16 : len(groups) * 16 + 16, :] = base
+            bases[...] = base.astype(F32)
         for i, g in enumerate(groups):
-            out[n, i * 16 : (i + 1) * 16, :] = (work[g * 16 : (g + 1) * 16, :] - base[i : i + 1, :]).astype(BF16)
+            out[n, i * 16 : (i + 1) * 16, :] = (work[g * 16 : (g + 1) * 16, :] - bases[g : g + 1, :]).astype(BF16)
 
     def collect(part_of):
         groups, code = parts[part_of], code_in[part_of]
@@ -504,10 +538,13 @@
             def _():
                 c_copy(part_of, n, n).wait_recv()
                 with jax.named_scope("add"):
-                    base = code[n, len(groups) * 16 : len(groups) * 16 + 16, :].astype(F32)
+                    if part_of == 2:
+                        base = code[n, 128:144, :].astype(F32)
+                    else:
+                        base = code_in[0][n, 64:80, :].astype(F32)
                     for i, g in enumerate(groups):
                         rows = slice(g * 16, (g + 1) * 16)
-                        acc[rows, :] += code[n, i * 16 : (i + 1) * 16, :].astype(F32) + base[i : i + 1, :]
+                        acc[rows, :] += code[n, i * 16 : (i + 1) * 16, :].astype(F32) + base[g : g + 1, :]
 
     def update(part_of):
         for g in parts[part_of]:
@@ -516,6 +553,8 @@
 
     def sent():
         around(everyone, lambda m: e_copy(0, m, 26 - m).wait_send())
+        for it in range(ITERS):
+            with_mate(lambda up: mate_rims(it, up).wait_send())
         for it in range(1, ITERS):
             around(everyone, lambda m: e_copy(it, m, 26 - m).wait_send())
             around(sides, lambda m: middle_copy(m, 26 - m).wait_send())
@@ -542,8 +581,11 @@
     for it in range(ITERS):
         if it > 0:
             with jax.named_scope("wait estimate 2"):
-                wait_estimate(it, everyone)
+                wait_estimate(it, sides)
+                with_mate(lambda up: mate_rims(it, up).start())
+                wait_estimate(it, rims)
                 around(sides, lambda m: middle_copy(m, m).wait_recv())
+                with_mate(lambda up: mate_rims(it, not up).wait_recv())
             with jax.named_scope("blur 2"):
                 blur(it)
         with jax.named_scope("quotients"):
@@ -641,13 +683,14 @@
             pltpu.VMEM((2, 128, 256), F32),
             pltpu.VMEM((256, 128), F32),
             pltpu.VMEM((128, 256), F32),
-            *[pltpu.VMEM((9, rows, 256), BF16) for rows in (80, 80, 144) * 2],
+            pltpu.VMEM((16, 256), F32),
+            *[pltpu.VMEM((9, rows, 256), BF16) for rows in (80, 64, 144) * 2],
             dma((16,)), dma((16,)),
             dma((2, 16)), dma((2, 4)),
             dma((ITERS, 27)), dma((ITERS, 27)),
             dma((9,)), dma((9,)),
             dma((3, 9)), dma((3, 9)),
-            dma(()), dma(()),
+            dma(()), dma(()), dma((ITERS,)), dma((ITERS,)),
         ],
         compiler_params=pltpu.CompilerParams(
             collective_id=0, has_side_effects=True, vmem_limit_bytes=55040 * 1024

time: 64.2 us -> 64.6 us (level)
  the two profiles are of different devices: /device:TPU:216 before, /device:TPU:168 now
where the time goes in v8:
time: 64.6 us; the launch traced here: 64.5 us
  Pallas kernels  63.1 us (98%)
  local copies, waits for them, and re-layouts  1.36 us (2%)
    pallas_call x1, Pallas kernels, per_device(): pl.pallas_call(functools.partial(kernel, sizes), out_shape=jax.ShapeDtype...  63.1 us
    unnamed x3, local copies, waits for them, and re-layouts  1.36 us

profile of v8, /device:TPU:168, one launch (start us, length us, event | category | flops | bytes accessed | tf_op | source)
XLA Modules:
  0.0 64.5 jit_solution(11683476963425561922)
XLA Ops:
  0.0 0.0 copy-start
  0.0 0.7 %copy-done = f32[6,3,31]{2,1,0:T(4,128)S(1)} copy-done((f32[6,3,31]{2,1,0:T(4,128)S(1)}, f32[6,3,31]{2,1,0:T(4,128)}, u32[]{:S(2)}) %copy-start) | copy-done | bytes 2256
  0.7 63.1 %shard_map.37 = f32[256,128]{1,0:T(8,128)S(1)} custom-call(bf16[6,32,4,256]{3,2,1,0:T(4,128)(2,1)} %cam_hbm.1, f32[256,128]{1,0:T(8,128)} %bitcast.3, f32[6,3,31]{2,1,0:T(4,128)S(1)} %copy-done), custom_call_target="tpu_custom_call" | custom-call | tf_op jit(solution)/shard_map/pallas_call | solution.py:650
  63.8 0.7 %copy.5 = f32[16,16,128]{2,1,0:T(8,128)} copy(f32[16,16,128]{2,1,0:T(8,128)S(1)} %bitcast.2) | data formatting | bytes 262144
Async XLA Ops:
  0.0 0.7 %copy-start = (f32[6,3,31]{2,1,0:T(4,128)S(1)}, f32[6,3,31]{2,1,0:T(4,128)}, u32[]{:S(2)}) copy-start(f32[6,3,31]{2,1,0:T(4,128)} %taps_hbm.1) | copy-start | bytes 6700

commit v9 on v8

--- a/solution.py
+++ b/solution.py
@@ -277,28 +277,31 @@
     with jax.named_scope("send estimate"):
         send_estimate(0, everyone)
 
+    def turn(s):
+        return (gx + 8 + s) & 15
+
     with jax.named_scope("send camera"):
-        @pl.when(part_z == gz)
-        def _():
-            cam_in[slot] = cam_out[gx]
-
-        others(16, target, lambda a: cam_copy(a, slot).start())
-
         @pl.when(gives_low)
         def _():
+            others(16, lambda s: low_target(turn(s)), lambda s: rim_copy(False, turn(s), gz).start())
+
             @pl.when(part_z + 1 == gz)
             def _():
                 rim_in[0, gz] = cam_out[gx, :, 16:32, :]
 
-            others(16, low_target, lambda a: rim_copy(False, a, gz).start())
-
         @pl.when(gives_high)
         def _():
+            others(16, lambda s: high_target(turn(s)), lambda s: rim_copy(True, turn(s), gz).start())
+
             @pl.when(part_z - 1 == gz)
             def _():
                 rim_in[1, gz] = cam_out[gx, :, 0:16, :]
 
-            others(16, high_target, lambda a: rim_copy(True, a, gz).start())
+        others(16, lambda s: target(turn(s)), lambda s: cam_copy(turn(s), slot).start())
+
+        @pl.when(part_z == gz)
+        def _():
+            cam_in[slot] = cam_out[gx]
 
     fetch[2].wait()
     with jax.named_scope("taps"):

time: 64.6 us -> 64.2 us (level)
  no operation moved by 1% of the time
where the time goes in v9:
time: 64.2 us; the launch traced here: 64 us
  Pallas kernels  62.7 us (98%)
  local copies, waits for them, and re-layouts  1.36 us (2%)
    pallas_call x1, Pallas kernels, per_device(): pl.pallas_call(functools.partial(kernel, sizes), out_shape=jax.ShapeDtype...  62.7 us
    unnamed x3, local copies, waits for them, and re-layouts  1.36 us

profile of v9, /device:TPU:168, one launch (start us, length us, event | category | flops | bytes accessed | tf_op | source)
XLA Modules:
  0.0 64.0 jit_solution(5367484336458465706)
XLA Ops:
  0.0 0.0 copy-start
  0.0 0.7 %copy-done = f32[6,3,31]{2,1,0:T(4,128)S(1)} copy-done((f32[6,3,31]{2,1,0:T(4,128)S(1)}, f32[6,3,31]{2,1,0:T(4,128)}, u32[]{:S(2)}) %copy-start) | copy-done | bytes 2256
  0.7 62.7 %shard_map.37 = f32[256,128]{1,0:T(8,128)S(1)} custom-call(bf16[6,32,4,256]{3,2,1,0:T(4,128)(2,1)} %cam_hbm.1, f32[256,128]{1,0:T(8,128)} %bitcast.3, f32[6,3,31]{2,1,0:T(4,128)S(1)} %copy-done), custom_call_target="tpu_custom_call" | custom-call | tf_op jit(solution)/shard_map/pallas_call | solution.py:653
  63.4 0.7 %copy.5 = f32[16,16,128]{2,1,0:T(8,128)} copy(f32[16,16,128]{2,1,0:T(8,128)S(1)} %bitcast.2) | data formatting | bytes 262144
Async XLA Ops:
  0.0 0.7 %copy-start = (f32[6,3,31]{2,1,0:T(4,128)S(1)}, f32[6,3,31]{2,1,0:T(4,128)}, u32[]{:S(2)}) copy-start(f32[6,3,31]{2,1,0:T(4,128)} %taps_hbm.1) | copy-start | bytes 6700

commit v10 on v5

--- a/solution.py
+++ b/solution.py
@@ -383,12 +383,14 @@
         value = scale[row : row + 1, :]
         return jnp.concatenate([value, value], axis=1)
 
+    def spread(it, first, last):
+        for v in range(VIEWS):
+            u = dot(ext[it, first:last, :], kf[v])
+            high = u.astype(BF16)
+            ubuf[v, first:last, 0:256] = high
+            ubuf[v, first:last, 256:512] = (u - high.astype(F32)).astype(BF16)
+
     def blur(it):
-        for v in range(VIEWS):
-            u = dot(ext[it], kf[v])
-            high = u.astype(BF16)
-            ubuf[v, 0:192, 0:256] = high
-            ubuf[v, 0:192, 256:512] = (u - high.astype(F32)).astype(BF16)
         for v in range(VIEWS):
             halves = dot(bzf[v].astype(BF16), ubuf[v])
             inverse[v] = factor(v) / (halves[:, 0:256] + halves[:, 256:512])
@@ -404,6 +406,7 @@
     with jax.named_scope("wait estimate"):
         wait_estimate(0, everyone)
     with jax.named_scope("blur"):
+        spread(0, 0, 192)
         blur(0)
 
     def mate_copy(first, to):
@@ -542,8 +545,11 @@
     for it in range(ITERS):
         if it > 0:
             with jax.named_scope("wait estimate 2"):
-                wait_estimate(it, everyone)
+                wait_estimate(it, sides)
                 around(sides, lambda m: middle_copy(m, m).wait_recv())
+                spread(it, 0, 128)
+                wait_estimate(it, rims)
+                spread(it, 128, 192)
             with jax.named_scope("blur 2"):
                 blur(it)
         with jax.named_scope("quotients"):

time: 64.2 us -> 65 us (1.012)
  the two profiles are of different devices: /device:TPU:216 before, /device:TPU:248 now
where the time goes in v10:
time: 65 us; the launch traced here: 64.8 us
  Pallas kernels  63.5 us (98%)
  local copies, waits for them, and re-layouts  1.36 us (2%)
    pallas_call x1, Pallas kernels, per_device(): pl.pallas_call(functools.partial(kernel, sizes), out_shape=jax.ShapeDtype...  63.5 us
    unnamed x3, local copies, waits for them, and re-layouts  1.36 us

profile of v10, /device:TPU:248, one launch (start us, length us, event | category | flops | bytes accessed | tf_op | source)
XLA Modules:
  0.0 64.8 jit_solution(14649494674979216804)
XLA Ops:
  0.0 0.0 copy-start
  0.0 0.7 %copy-done = f32[6,3,31]{2,1,0:T(4,128)S(1)} copy-done((f32[6,3,31]{2,1,0:T(4,128)S(1)}, f32[6,3,31]{2,1,0:T(4,128)}, u32[]{:S(2)}) %copy-start) | copy-done | bytes 2256
  0.7 63.5 %shard_map.37 = f32[256,128]{1,0:T(8,128)S(1)} custom-call(bf16[6,32,4,256]{3,2,1,0:T(4,128)(2,1)} %cam_hbm.1, f32[256,128]{1,0:T(8,128)} %bitcast.3, f32[6,3,31]{2,1,0:T(4,128)S(1)} %copy-done), custom_call_target="tpu_custom_call" | custom-call | tf_op jit(solution)/shard_map/pallas_call | solution.py:614
  64.2 0.7 %copy.5 = f32[16,16,128]{2,1,0:T(8,128)} copy(f32[16,16,128]{2,1,0:T(8,128)S(1)} %bitcast.2) | data formatting | bytes 262144
Async XLA Ops:
  0.0 0.7 %copy-start = (f32[6,3,31]{2,1,0:T(4,128)S(1)}, f32[6,3,31]{2,1,0:T(4,128)}, u32[]{:S(2)}) copy-start(f32[6,3,31]{2,1,0:T(4,128)} %taps_hbm.1) | copy-start | bytes 6700
